TPU v7x, 1024 devices: a whole 4x8x16 slice. The times are simulated.
1024 devices in a mesh: gx: 64 (over z_lo, y), gy: 16 (over x, z_hi, core).
Axes of the slice: x: 4, y: 8, z: 16 (z_hi: 2, z_lo: 8; z = z_hi * 8 + z_lo), core: 2. Of those that a mesh axis runs over, the one named last changes fastest.
Arguments:
- positions: float32 [3, 32768], P(None, ('gx', 'gy')), may hold values from -4 to 4
- species: int32 [32768], P(('gx', 'gy')), may hold values from 0 to 7
- atom_count: int32 [1024], P(('gx', 'gy')), may hold values from 10 to 32, as said below
- send_list: int32 [1024, 8, 4], P(('gx', 'gy')), may hold values from 0 to 31, as said below
- edges: int32 [1024, 2, 256], P(('gx', 'gy')), may hold values from 0 to 63, as said below
- centre_embed: float32 [512, 8], replicated, may hold values from -3 to 3
- neighbour_embed: float32 [512, 8], replicated, may hold values from -3 to 3
- radial_weight: float32 [512, 8], replicated, may hold values from -2 to 2
- env_weight: float32 [2, 64, 512], replicated, may hold values from -0.25 to 0.25
- latent_weight: float32 [2, 512, 704], replicated, may hold values from -0.21875 to 0.21875
- out_weight: float32 [512, 512], replicated, may hold values from -0.25 to 0.25
- head_weight: float32 [2, 512], replicated, may hold values from -0.25 to 0.25
Outputs:
- atom_energy: float32 [32768], P(('gx', 'gy'))
- forces: float32 [3, 32768], P(None, ('gx', 'gy'))
Inputs may be any that keep to these rules, and one draw needn't show every extreme that they name: Device p's live atoms are its slots 0 to atom_count[p] - 1, the rest are padding; its live edges are its first 8 atom_count[p] edge slots. send_list[p, k, g] is a live atom of device p; the 4 atoms of one (p, k) are distinct and are sent to the device at offset k. `edges`: row 0 is a live atom slot of the device; row 1 is a live atom slot other than the centre, or a ghost slot 32 + k * 4 + g.
All inputs are finite; a program needn't handle non-finite values.
Results may differ from a plain program's by a relative error of at most 0.00025.
Values sent between devices are 32-bit elements; how exact they have to be, the bound alone decides.
A program may use at most 32 MiB of HBM per device.

v0:
```python
import math

import jax
import jax.numpy as jnp
from jax import lax
from jax.sharding import PartitionSpec as P

offset_x = (-1, -1, -1, 0, 0, 1, 1, 1)
offset_y = (-1, 0, 1, -1, 1, -1, 0, 1)
highest = lax.Precision.HIGHEST


def extended(value, sides, width):
    for axis, dim in sides:
        peers, length = (lax.axis_size(axis), value.shape[dim])
        up = [(i, (i + 1) % peers) for i in range(peers)]
        down = [(j, i) for i, j in up]
        last = lax.slice_in_dim(value, length - width, length, axis=dim)
        initial = lax.slice_in_dim(value, 0, width, axis=dim)
        before = lax.ppermute(last, axis, up)
        after = lax.ppermute(initial, axis, down)
        value = jnp.concatenate([before, value, after], axis=dim)
    return value


def parity():
    return jnp.array([1.0, -1.0, -1.0, -1.0, 1.0, 1.0, 1.0, 1.0, 1.0], dtype=jnp.float32)


def harmonics(unit):
    root = math.sqrt(3.0)
    along_x, along_y, along_z = (unit[0], unit[1], unit[2])
    return jnp.stack(
        [
            jnp.ones_like(along_x),
            along_x,
            along_y,
            along_z,
            root * along_x * along_y,
            root * along_y * along_z,
            0.5 * (3.0 * along_z * along_z - 1.0),
            root * along_x * along_z,
            0.5 * root * (along_x * along_x - along_y * along_y),
        ]
    )


def geometry(start, finish, count_basis):
    offset = finish - start
    squared = jnp.sum(offset * offset, axis=0)
    unit = offset / jnp.sqrt(1.0 + squared)
    length = jnp.sqrt(squared)
    centres = 0.5 * jnp.arange(count_basis, dtype=jnp.float32)
    basis = jnp.exp(-2.0 * (length[None, :] - centres[:, None]) ** 2)
    return (unit, basis, harmonics(unit))


def refine(hidden, env_centre, env_other, harm, weight):
    sign = parity()[None, :, None]
    product = (env_centre + env_other * sign) * harm[None]
    scalars = jnp.concatenate(
        [hidden, product[:, 0], jnp.sum(product[:, 1:4], axis=1), jnp.sum(product[:, 4:9], axis=1)],
        axis=0,
    )
    return hidden + jax.nn.silu(jnp.dot(weight, scalars, precision=highest))


def to_grid(items):
    padding = jnp.zeros_like(items[:1])
    joined = jnp.concatenate([items[:4], padding, items[4:]], axis=0)
    return joined.reshape((3, 3) + items.shape[1:])


def deliver(items, backward):
    grid = to_grid(items)
    if backward:
        padded = extended(grid, (("gx", 0), ("gy", 1)), 1)
    else:
        padded = extended(grid, (("gx", 0), ("gy", 1)), 1)
    return jnp.stack(
        [padded[2 + 2 * offset_x[direction], 2 + 2 * offset_y[direction]] for direction in range(8)]
    )


def flatten(items):
    return items.transpose(1, 0, 2).reshape(items.shape[1], -1)


def spread(values, sends):
    rows = values.shape[0]
    picked = jnp.take(values, sends, axis=1).reshape(rows, 8, -1).transpose(1, 0, 2)
    ghosts = deliver(picked, False)
    return jnp.concatenate([values, flatten(ghosts)], axis=1)


def collect(partial_value, sends, atoms):
    rows = partial_value.shape[0]
    own = partial_value[:, :atoms]
    ghost_items = partial_value[:, atoms:].reshape(rows, 8, -1).transpose(1, 0, 2)
    returned = deliver(ghost_items, True)
    return own.at[:, sends].add(flatten(returned))


def local(
    positions,
    species,
    atom_count,
    send_list,
    edges,
    centre_embed,
    neighbour_embed,
    radial_weight,
    env_weight,
    latent_weight,
    out_weight,
    head_weight,
):
    atoms = positions.shape[1]
    channels = env_weight.shape[1]
    count_edges = edges.shape[2]
    sends = send_list[0].reshape(-1)
    slots_all = atoms + sends.shape[0]
    centre = edges[0, 0]
    other = edges[0, 1]
    per_atom = count_edges // atoms
    live = (jnp.arange(count_edges, dtype=jnp.int32) < per_atom * atom_count[0]).astype(jnp.float32)
    coords = jnp.concatenate([positions, species.astype(jnp.float32)[None]], axis=0)
    pool = spread(coords, sends)
    start = pool[:, centre]
    finish = pool[:, other]
    unit, basis, harm = geometry(start[:3], finish[:3], radial_weight.shape[1])
    kinds = jnp.arange(centre_embed.shape[1], dtype=jnp.float32)[:, None]
    onehot_centre = (start[3][None, :] == kinds).astype(jnp.float32)
    onehot_other = (finish[3][None, :] == kinds).astype(jnp.float32)
    inner = jnp.dot(radial_weight, basis, precision=highest)
    inner = inner + jnp.dot(centre_embed, onehot_centre, precision=highest)
    inner = inner + jnp.dot(neighbour_embed, onehot_other, precision=highest)
    hidden = jax.nn.silu(inner)
    parity_rows = jnp.tile(parity(), channels)[:, None]
    for layer in range(env_weight.shape[0]):
        weights_e = jnp.dot(env_weight[layer], hidden, precision=highest)
        contrib = (weights_e[:, None, :] * harm[None]).reshape(channels * 9, count_edges) * (
            live * 0.25
        )
        partial_value = jnp.zeros((channels * 9, slots_all), jnp.float32)
        partial_value = (
            partial_value.at[:, centre].add(contrib).at[:, other].add(contrib * parity_rows)
        )
        env_own = collect(partial_value, sends, atoms)
        env_pool = spread(env_own, sends)
        env_centre = env_pool[:, centre].reshape(channels, 9, count_edges)
        env_other = env_pool[:, other].reshape(channels, 9, count_edges)
        hidden = refine(hidden, env_centre, env_other, harm, latent_weight[layer])
    latent = jax.nn.silu(jnp.dot(out_weight, hidden, precision=highest))
    heads = jnp.dot(head_weight, latent, precision=highest)
    energy_e = 0.5 * heads[0] * live
    push = heads[1] * live * unit
    partial_value = jnp.zeros((4, slots_all), jnp.float32)
    partial_value = partial_value.at[:, centre].add(jnp.concatenate([energy_e[None], push], axis=0))
    partial_value = partial_value.at[:, other].add(jnp.concatenate([energy_e[None], -push], axis=0))
    totals = collect(partial_value, sends, atoms)
    return (totals[0], totals[1:4])


def solution(mesh):
    placed = (
        P(None, ("gx", "gy")),
        P(("gx", "gy")),
        P(("gx", "gy")),
        P(("gx", "gy"), None, None),
        P(("gx", "gy"), None, None),
        P(),
        P(),
        P(),
        P(),
        P(),
        P(),
        P(),
    )
    return jax.shard_map(
        local,
        mesh=mesh,
        in_specs=placed,
        out_specs=(P(("gx", "gy")), P(None, ("gx", "gy"))),
        check_vma=False,
    )
```

profile of v0, /device:TPU:1, one launch (start us, length us, event | category | flops | bytes accessed | tf_op | source)
XLA Modules:
  0.0 299.0 jit_solution(5126855115097364426)
XLA Ops:
  5.3 19.8 %collective-permute-start.1 = (f32[1,3,4,4]{3,2,1,0:T(4,128)S(1)}, f32[1,3,4,4]{3,2,1,0:T(4,128)S(1)}, u32[]{:S(2)}, u32[]{:S(2)}) collective-permute-start(f32[1,3,4,4]{3,2,1,0:T(4,128)S(1)} %bitcast.394), channel_id=1, source_target_pairs={{16,0},{32,16},{48,32},{64,48},{80,64},{96,80},{112,96},{128,112},... | collective-permute-start | bytes 584 | tf_op jit(solution)/shard_map/ppermute | solution.py:21
  28.0 10.2 %collective-permute-done = f32[1,3,4,4]{3,2,1,0:T(4,128)S(1)} collective-permute-done((f32[1,3,4,4]{3,2,1,0:T(4,128)S(1)}, f32[1,3,4,4]{3,2,1,0:T(4,128)S(1)}, u32[]{:S(2)}, u32[]{:S(2)}) %collective-permute-start) | collective-permute-done | bytes 224 | tf_op jit(solution)/shard_map/ppermute | solution.py:20
  38.2 13.6 %collective-permute-start.2 = (f32[5,1,4,4]{3,2,1,0:T(4,128)S(1)}, f32[5,1,4,4]{3,2,1,0:T(4,128)S(1)}, u32[]{:S(2)}, u32[]{:S(2)}) collective-permute-start(f32[5,1,4,4]{3,2,1,0:T(4,128)S(1)} %get-tuple-element.50), channel_id=1, source_target_pairs={{0,1},{1,2},{2,3},{3,4},{4,5},{5,6},{6,7},{7,8},{8,9},{9,10},{10,1... | collective-permute-start | bytes 968 | tf_op jit(solution)/shard_map/ppermute | solution.py:20
  52.6 1.9 collective-permute-start.3
  54.6 11.7 %collective-permute-done.3 = f32[5,1,4,4]{3,2,1,0:T(4,128)S(1)} collective-permute-done((f32[5,1,4,4]{3,2,1,0:T(4,128)S(1)}, f32[5,1,4,4]{3,2,1,0:T(4,128)S(1)}, u32[]{:S(2)}, u32[]{:S(2)}) %collective-permute-start.3) | collective-permute-done | bytes 352 | tf_op jit(solution)/shard_map/ppermute | solution.py:21
  75.0 2.3 scatter_custom_fusion
  77.3 2.3 scatter_fusion
  81.6 12.1 %collective-permute-start.5 = (f32[1,3,576,4]{2,3,1,0:T(4,128)S(1)}, f32[1,3,576,4]{2,3,1,0:T(4,128)S(1)}, u32[]{:S(2)}, u32[]{:S(2)}) collective-permute-start(f32[1,3,576,4]{2,3,1,0:T(4,128)S(1)} %get-tuple-element.42), channel_id=1, source_target_pairs={{16,0},{32,16},{48,32},{64,48},{80,64},{96,80},{112,96},{128,112},... | collective-permute-start | bytes 82952 | tf_op jit(solution)/shard_map/ppermute | solution.py:21
  94.7 3.1 %collective-permute-start.6 = (f32[5,1,576,4]{2,3,1,0:T(4,128)S(1)}, f32[5,1,576,4]{2,3,1,0:T(4,128)S(1)}, u32[]{:S(2)}, u32[]{:S(2)}) collective-permute-start(f32[5,1,576,4]{2,3,1,0:T(4,128)S(1)} %get-tuple-element.28), channel_id=1, source_target_pairs={{0,1},{1,2},{2,3},{3,4},{4,5},{5,6},{6,7},{7,8},{8,9},{9,10},{10,1... | collective-permute-start | bytes 138248 | tf_op jit(solution)/shard_map/ppermute | solution.py:20
  99.8 12.2 %collective-permute-done.7 = f32[5,1,576,4]{2,3,1,0:T(4,128)S(1)} collective-permute-done((f32[5,1,576,4]{2,3,1,0:T(4,128)S(1)}, f32[5,1,576,4]{2,3,1,0:T(4,128)S(1)}, u32[]{:S(2)}, u32[]{:S(2)}) %collective-permute-start.7) | collective-permute-done | bytes 46112 | tf_op jit(solution)/shard_map/ppermute | solution.py:21
  115.6 12.8 %collective-permute-start.9 = (f32[1,3,576,4]{2,3,1,0:T(4,128)S(1)}, f32[1,3,576,4]{2,3,1,0:T(4,128)S(1)}, u32[]{:S(2)}, u32[]{:S(2)}) collective-permute-start(f32[1,3,576,4]{2,3,1,0:T(4,128)S(1)} %get-tuple-element.38), channel_id=1, source_target_pairs={{16,0},{32,16},{48,32},{64,48},{80,64},{96,80},{112,96},{128,112},... | collective-permute-start | bytes 82952 | tf_op jit(solution)/shard_map/ppermute | solution.py:21
  129.4 2.6 collective-permute-start.10
  132.0 2.1 collective-permute-start.11
  134.2 12.0 %collective-permute-done.11 = f32[5,1,576,4]{2,3,1,0:T(4,128)S(1)} collective-permute-done((f32[5,1,576,4]{2,3,1,0:T(4,128)S(1)}, f32[5,1,576,4]{2,3,1,0:T(4,128)S(1)}, u32[]{:S(2)}, u32[]{:S(2)}) %collective-permute-start.11) | collective-permute-done | bytes 46112 | tf_op jit(solution)/shard_map/ppermute | solution.py:21
  147.4 2.0 gather_fusion.3
  163.1 2.3 scatter_custom_fusion.3
  165.4 2.3 scatter_fusion.1
  169.7 12.7 %collective-permute-start.13 = (f32[1,3,576,4]{2,3,1,0:T(4,128)S(1)}, f32[1,3,576,4]{2,3,1,0:T(4,128)S(1)}, u32[]{:S(2)}, u32[]{:S(2)}) collective-permute-start(f32[1,3,576,4]{2,3,1,0:T(4,128)S(1)} %get-tuple-element.34), channel_id=1, source_target_pairs={{16,0},{32,16},{48,32},{64,48},{80,64},{96,80},{112,96},{128,112},... | collective-permute-start | bytes 82952 | tf_op jit(solution)/shard_map/ppermute | solution.py:21
  183.4 2.7 collective-permute-start.14
  188.1 12.2 %collective-permute-done.15 = f32[5,1,576,4]{2,3,1,0:T(4,128)S(1)} collective-permute-done((f32[5,1,576,4]{2,3,1,0:T(4,128)S(1)}, f32[5,1,576,4]{2,3,1,0:T(4,128)S(1)}, u32[]{:S(2)}, u32[]{:S(2)}) %collective-permute-start.15) | collective-permute-done | bytes 46112 | tf_op jit(solution)/shard_map/ppermute | solution.py:21
  203.9 12.7 %collective-permute-start.17 = (f32[1,3,576,4]{2,3,1,0:T(4,128)S(1)}, f32[1,3,576,4]{2,3,1,0:T(4,128)S(1)}, u32[]{:S(2)}, u32[]{:S(2)}) collective-permute-start(f32[1,3,576,4]{2,3,1,0:T(4,128)S(1)} %get-tuple-element.30), channel_id=1, source_target_pairs={{16,0},{32,16},{48,32},{64,48},{80,64},{96,80},{112,96},{128,112},... | collective-permute-start | bytes 82952 | tf_op jit(solution)/shard_map/ppermute | solution.py:21
  217.6 2.7 collective-permute-start.18
  220.4 2.1 collective-permute-start.19
  222.6 12.0 %collective-permute-done.19 = f32[5,1,576,4]{2,3,1,0:T(4,128)S(1)} collective-permute-done((f32[5,1,576,4]{2,3,1,0:T(4,128)S(1)}, f32[5,1,576,4]{2,3,1,0:T(4,128)S(1)}, u32[]{:S(2)}, u32[]{:S(2)}) %collective-permute-start.19) | collective-permute-done | bytes 46112 | tf_op jit(solution)/shard_map/ppermute | solution.py:21
  235.8 2.0 gather_fusion.5
  251.5 2.0 scatter_fusion.2
  253.7 12.6 %collective-permute-start.21 = (f32[1,3,4,4]{3,2,1,0:T(4,128)S(1)}, f32[1,3,4,4]{3,2,1,0:T(4,128)S(1)}, u32[]{:S(2)}, u32[]{:S(2)}) collective-permute-start(f32[1,3,4,4]{3,2,1,0:T(4,128)S(1)} %bitcast.397), channel_id=1, source_target_pairs={{16,0},{32,16},{48,32},{64,48},{80,64},{96,80},{112,96},{128,112},... | collective-permute-start | bytes 584 | tf_op jit(solution)/shard_map/ppermute | solution.py:21
  266.3 1.9 collective-permute-start.20
  268.3 11.1 %collective-permute-done.20 = f32[1,3,4,4]{3,2,1,0:T(4,128)S(1)} collective-permute-done((f32[1,3,4,4]{3,2,1,0:T(4,128)S(1)}, f32[1,3,4,4]{3,2,1,0:T(4,128)S(1)}, u32[]{:S(2)}, u32[]{:S(2)}) %collective-permute-start.20) | collective-permute-done | bytes 224 | tf_op jit(solution)/shard_map/ppermute | solution.py:20
  279.4 3.3 %collective-permute-start.22 = (f32[5,1,4,4]{3,2,1,0:T(4,128)S(1)}, f32[5,1,4,4]{3,2,1,0:T(4,128)S(1)}, u32[]{:S(2)}, u32[]{:S(2)}) collective-permute-start(f32[5,1,4,4]{3,2,1,0:T(4,128)S(1)} %get-tuple-element.48), channel_id=1, source_target_pairs={{0,1},{1,2},{2,3},{3,4},{4,5},{5,6},{6,7},{7,8},{8,9},{9,10},{10,1... | collective-permute-start | bytes 968 | tf_op jit(solution)/shard_map/ppermute | solution.py:20
  282.7 3.2 %collective-permute-start.23 = (f32[5,1,4,4]{3,2,1,0:T(4,128)S(1)}, f32[5,1,4,4]{3,2,1,0:T(4,128)S(1)}, u32[]{:S(2)}, u32[]{:S(2)}) collective-permute-start(f32[5,1,4,4]{3,2,1,0:T(4,128)S(1)} %get-tuple-element.47), channel_id=1, source_target_pairs={{1,0},{2,1},{3,2},{4,3},{5,4},{6,5},{7,6},{8,7},{9,8},{10,9},{11,1... | collective-permute-start | bytes 968 | tf_op jit(solution)/shard_map/ppermute | solution.py:21
  286.0 10.7 %collective-permute-done.23 = f32[5,1,4,4]{3,2,1,0:T(4,128)S(1)} collective-permute-done((f32[5,1,4,4]{3,2,1,0:T(4,128)S(1)}, f32[5,1,4,4]{3,2,1,0:T(4,128)S(1)}, u32[]{:S(2)}, u32[]{:S(2)}) %collective-permute-start.23) | collective-permute-done | bytes 352 | tf_op jit(solution)/shard_map/ppermute | solution.py:21
  (245 shorter events, 67.4 us)
Async XLA Ops:
  0.6 247.3 %copy-start = (f32[512,512]{1,0:T(8,128)S(1)}, f32[512,512]{1,0:T(8,128)}, u32[]{:S(2)}) copy-start(f32[512,512]{1,0:T(8,128)} %param.27) | copy-start | bytes 3145732
  0.6 69.8 %copy-start.9 = (f32[512,8]{0,1:T(8,128)S(1)}, f32[512,8]{0,1:T(8,128)}, u32[]{:S(2)}) copy-start(f32[512,8]{0,1:T(8,128)} %param.22) | copy-start | bytes 49156
  5.3 22.7 %collective-permute-start.1 = (f32[1,3,4,4]{3,2,1,0:T(4,128)S(1)}, f32[1,3,4,4]{3,2,1,0:T(4,128)S(1)}, u32[]{:S(2)}, u32[]{:S(2)}) collective-permute-start(f32[1,3,4,4]{3,2,1,0:T(4,128)S(1)} %bitcast.394), channel_id=1, source_target_pairs={{16,0},{32,16},{48,32},{64,48},{80,64},{96,80},{112,96},{128,112},... | collective-permute-start | bytes 584 | tf_op jit(solution)/shard_map/ppermute | solution.py:21
  25.1 13.1 %collective-permute-start = (f32[1,3,4,4]{3,2,1,0:T(4,128)S(1)}, f32[1,3,4,4]{3,2,1,0:T(4,128)S(1)}, u32[]{:S(2)}, u32[]{:S(2)}) collective-permute-start(f32[1,3,4,4]{3,2,1,0:T(4,128)S(1)} %bitcast.395), channel_id=1, source_target_pairs={{0,16},{16,32},{32,48},{48,64},{64,80},{80,96},{96,112},{112,128},... | collective-permute-start | bytes 584 | tf_op jit(solution)/shard_map/ppermute | solution.py:20
  27.9 43.0 %copy-start.11 = (f32[512,8]{0,1:T(8,128)S(1)}, f32[512,8]{0,1:T(8,128)}, u32[]{:S(2)}) copy-start(f32[512,8]{0,1:T(8,128)} %param.23) | copy-start | bytes 49156
  38.2 16.3 %collective-permute-start.2 = (f32[5,1,4,4]{3,2,1,0:T(4,128)S(1)}, f32[5,1,4,4]{3,2,1,0:T(4,128)S(1)}, u32[]{:S(2)}, u32[]{:S(2)}) collective-permute-start(f32[5,1,4,4]{3,2,1,0:T(4,128)S(1)} %get-tuple-element.50), channel_id=1, source_target_pairs={{0,1},{1,2},{2,3},{3,4},{4,5},{5,6},{6,7},{7,8},{8,9},{9,10},{10,1... | collective-permute-start | bytes 968 | tf_op jit(solution)/shard_map/ppermute | solution.py:20
  52.6 13.7 %collective-permute-start.3 = (f32[5,1,4,4]{3,2,1,0:T(4,128)S(1)}, f32[5,1,4,4]{3,2,1,0:T(4,128)S(1)}, u32[]{:S(2)}, u32[]{:S(2)}) collective-permute-start(f32[5,1,4,4]{3,2,1,0:T(4,128)S(1)} %get-tuple-element.49), channel_id=1, source_target_pairs={{1,0},{2,1},{3,2},{4,3},{5,4},{6,5},{7,6},{8,7},{9,8},{10,9},{11,1... | collective-permute-start | bytes 968 | tf_op jit(solution)/shard_map/ppermute | solution.py:21
  79.7 14.1 %collective-permute-start.4 = (f32[1,3,576,4]{2,3,1,0:T(4,128)S(1)}, f32[1,3,576,4]{2,3,1,0:T(4,128)S(1)}, u32[]{:S(2)}, u32[]{:S(2)}) collective-permute-start(f32[1,3,576,4]{2,3,1,0:T(4,128)S(1)} %get-tuple-element.41), channel_id=1, source_target_pairs={{0,16},{16,32},{32,48},{48,64},{64,80},{80,96},{96,112},{112,128},... | collective-permute-start | bytes 82952 | tf_op jit(solution)/shard_map/ppermute | solution.py:20
  81.6 13.1 %collective-permute-start.5 = (f32[1,3,576,4]{2,3,1,0:T(4,128)S(1)}, f32[1,3,576,4]{2,3,1,0:T(4,128)S(1)}, u32[]{:S(2)}, u32[]{:S(2)}) collective-permute-start(f32[1,3,576,4]{2,3,1,0:T(4,128)S(1)} %get-tuple-element.42), channel_id=1, source_target_pairs={{16,0},{32,16},{48,32},{64,48},{80,64},{96,80},{112,96},{128,112},... | collective-permute-start | bytes 82952 | tf_op jit(solution)/shard_map/ppermute | solution.py:21
  94.7 5.0 %collective-permute-start.6 = (f32[5,1,576,4]{2,3,1,0:T(4,128)S(1)}, f32[5,1,576,4]{2,3,1,0:T(4,128)S(1)}, u32[]{:S(2)}, u32[]{:S(2)}) collective-permute-start(f32[5,1,576,4]{2,3,1,0:T(4,128)S(1)} %get-tuple-element.28), channel_id=1, source_target_pairs={{0,1},{1,2},{2,3},{3,4},{4,5},{5,6},{6,7},{7,8},{8,9},{9,10},{10,1... | collective-permute-start | bytes 138248 | tf_op jit(solution)/shard_map/ppermute | solution.py:20
  97.8 14.2 %collective-permute-start.7 = (f32[5,1,576,4]{2,3,1,0:T(4,128)S(1)}, f32[5,1,576,4]{2,3,1,0:T(4,128)S(1)}, u32[]{:S(2)}, u32[]{:S(2)}) collective-permute-start(f32[5,1,576,4]{2,3,1,0:T(4,128)S(1)} %get-tuple-element.27), channel_id=1, source_target_pairs={{1,0},{2,1},{3,2},{4,3},{5,4},{6,5},{7,6},{8,7},{9,8},{10,9},{11,1... | collective-permute-start | bytes 138248 | tf_op jit(solution)/shard_map/ppermute | solution.py:21
  113.6 14.8 %collective-permute-start.8 = (f32[1,3,576,4]{2,3,1,0:T(4,128)S(1)}, f32[1,3,576,4]{2,3,1,0:T(4,128)S(1)}, u32[]{:S(2)}, u32[]{:S(2)}) collective-permute-start(f32[1,3,576,4]{2,3,1,0:T(4,128)S(1)} %get-tuple-element.37), channel_id=1, source_target_pairs={{0,16},{16,32},{32,48},{48,64},{64,80},{80,96},{96,112},{112,128},... | collective-permute-start | bytes 82952 | tf_op jit(solution)/shard_map/ppermute | solution.py:20
  115.6 13.7 %collective-permute-start.9 = (f32[1,3,576,4]{2,3,1,0:T(4,128)S(1)}, f32[1,3,576,4]{2,3,1,0:T(4,128)S(1)}, u32[]{:S(2)}, u32[]{:S(2)}) collective-permute-start(f32[1,3,576,4]{2,3,1,0:T(4,128)S(1)} %get-tuple-element.38), channel_id=1, source_target_pairs={{16,0},{32,16},{48,32},{64,48},{80,64},{96,80},{112,96},{128,112},... | collective-permute-start | bytes 82952 | tf_op jit(solution)/shard_map/ppermute | solution.py:21
  129.4 4.8 %collective-permute-start.10 = (f32[5,1,576,4]{2,3,1,0:T(4,128)S(1)}, f32[5,1,576,4]{2,3,1,0:T(4,128)S(1)}, u32[]{:S(2)}, u32[]{:S(2)}) collective-permute-start(f32[5,1,576,4]{2,3,1,0:T(4,128)S(1)} %get-tuple-element.26), channel_id=1, source_target_pairs={{0,1},{1,2},{2,3},{3,4},{4,5},{5,6},{6,7},{7,8},{8,9},{9,10},{10,1... | collective-permute-start | bytes 138248 | tf_op jit(solution)/shard_map/ppermute | solution.py:20
  132.0 14.1 %collective-permute-start.11 = (f32[5,1,576,4]{2,3,1,0:T(4,128)S(1)}, f32[5,1,576,4]{2,3,1,0:T(4,128)S(1)}, u32[]{:S(2)}, u32[]{:S(2)}) collective-permute-start(f32[5,1,576,4]{2,3,1,0:T(4,128)S(1)} %get-tuple-element.25), channel_id=1, source_target_pairs={{1,0},{2,1},{3,2},{4,3},{5,4},{6,5},{7,6},{8,7},{9,8},{10,9},{11,1... | collective-permute-start | bytes 138248 | tf_op jit(solution)/shard_map/ppermute | solution.py:21
  154.4 1.6 copy-start.10
  156.0 1.8 copy-start.3
  156.5 1.6 copy-start.6
  158.0 2.4 copy-start.8
  167.8 14.7 %collective-permute-start.12 = (f32[1,3,576,4]{2,3,1,0:T(4,128)S(1)}, f32[1,3,576,4]{2,3,1,0:T(4,128)S(1)}, u32[]{:S(2)}, u32[]{:S(2)}) collective-permute-start(f32[1,3,576,4]{2,3,1,0:T(4,128)S(1)} %get-tuple-element.33), channel_id=1, source_target_pairs={{0,16},{16,32},{32,48},{48,64},{64,80},{80,96},{96,112},{112,128},... | collective-permute-start | bytes 82952 | tf_op jit(solution)/shard_map/ppermute | solution.py:20
  169.7 13.6 %collective-permute-start.13 = (f32[1,3,576,4]{2,3,1,0:T(4,128)S(1)}, f32[1,3,576,4]{2,3,1,0:T(4,128)S(1)}, u32[]{:S(2)}, u32[]{:S(2)}) collective-permute-start(f32[1,3,576,4]{2,3,1,0:T(4,128)S(1)} %get-tuple-element.34), channel_id=1, source_target_pairs={{16,0},{32,16},{48,32},{64,48},{80,64},{96,80},{112,96},{128,112},... | collective-permute-start | bytes 82952 | tf_op jit(solution)/shard_map/ppermute | solution.py:21
  183.4 4.7 %collective-permute-start.14 = (f32[5,1,576,4]{2,3,1,0:T(4,128)S(1)}, f32[5,1,576,4]{2,3,1,0:T(4,128)S(1)}, u32[]{:S(2)}, u32[]{:S(2)}) collective-permute-start(f32[5,1,576,4]{2,3,1,0:T(4,128)S(1)} %get-tuple-element.24), channel_id=1, source_target_pairs={{0,1},{1,2},{2,3},{3,4},{4,5},{5,6},{6,7},{7,8},{8,9},{9,10},{10,1... | collective-permute-start | bytes 138248 | tf_op jit(solution)/shard_map/ppermute | solution.py:20
  186.1 14.1 %collective-permute-start.15 = (f32[5,1,576,4]{2,3,1,0:T(4,128)S(1)}, f32[5,1,576,4]{2,3,1,0:T(4,128)S(1)}, u32[]{:S(2)}, u32[]{:S(2)}) collective-permute-start(f32[5,1,576,4]{2,3,1,0:T(4,128)S(1)} %get-tuple-element.23), channel_id=1, source_target_pairs={{1,0},{2,1},{3,2},{4,3},{5,4},{6,5},{7,6},{8,7},{9,8},{10,9},{11,1... | collective-permute-start | bytes 138248 | tf_op jit(solution)/shard_map/ppermute | solution.py:21
  202.0 14.7 %collective-permute-start.16 = (f32[1,3,576,4]{2,3,1,0:T(4,128)S(1)}, f32[1,3,576,4]{2,3,1,0:T(4,128)S(1)}, u32[]{:S(2)}, u32[]{:S(2)}) collective-permute-start(f32[1,3,576,4]{2,3,1,0:T(4,128)S(1)} %get-tuple-element.29), channel_id=1, source_target_pairs={{0,16},{16,32},{32,48},{48,64},{64,80},{80,96},{96,112},{112,128},... | collective-permute-start | bytes 82952 | tf_op jit(solution)/shard_map/ppermute | solution.py:20
  203.9 13.7 %collective-permute-start.17 = (f32[1,3,576,4]{2,3,1,0:T(4,128)S(1)}, f32[1,3,576,4]{2,3,1,0:T(4,128)S(1)}, u32[]{:S(2)}, u32[]{:S(2)}) collective-permute-start(f32[1,3,576,4]{2,3,1,0:T(4,128)S(1)} %get-tuple-element.30), channel_id=1, source_target_pairs={{16,0},{32,16},{48,32},{64,48},{80,64},{96,80},{112,96},{128,112},... | collective-permute-start | bytes 82952 | tf_op jit(solution)/shard_map/ppermute | solution.py:21
  217.6 4.9 %collective-permute-start.18 = (f32[5,1,576,4]{2,3,1,0:T(4,128)S(1)}, f32[5,1,576,4]{2,3,1,0:T(4,128)S(1)}, u32[]{:S(2)}, u32[]{:S(2)}) collective-permute-start(f32[5,1,576,4]{2,3,1,0:T(4,128)S(1)} %get-tuple-element.22), channel_id=1, source_target_pairs={{0,1},{1,2},{2,3},{3,4},{4,5},{5,6},{6,7},{7,8},{8,9},{9,10},{10,1... | collective-permute-start | bytes 138248 | tf_op jit(solution)/shard_map/ppermute | solution.py:20
  220.4 14.2 %collective-permute-start.19 = (f32[5,1,576,4]{2,3,1,0:T(4,128)S(1)}, f32[5,1,576,4]{2,3,1,0:T(4,128)S(1)}, u32[]{:S(2)}, u32[]{:S(2)}) collective-permute-start(f32[5,1,576,4]{2,3,1,0:T(4,128)S(1)} %get-tuple-element.21), channel_id=1, source_target_pairs={{1,0},{2,1},{3,2},{4,3},{5,4},{6,5},{7,6},{8,7},{9,8},{10,9},{11,1... | collective-permute-start | bytes 138248 | tf_op jit(solution)/shard_map/ppermute | solution.py:21
  244.4 1.8 copy-start.4
  253.7 14.6 %collective-permute-start.21 = (f32[1,3,4,4]{3,2,1,0:T(4,128)S(1)}, f32[1,3,4,4]{3,2,1,0:T(4,128)S(1)}, u32[]{:S(2)}, u32[]{:S(2)}) collective-permute-start(f32[1,3,4,4]{3,2,1,0:T(4,128)S(1)} %bitcast.397), channel_id=1, source_target_pairs={{16,0},{32,16},{48,32},{64,48},{80,64},{96,80},{112,96},{128,112},... | collective-permute-start | bytes 584 | tf_op jit(solution)/shard_map/ppermute | solution.py:21
  266.3 13.1 %collective-permute-start.20 = (f32[1,3,4,4]{3,2,1,0:T(4,128)S(1)}, f32[1,3,4,4]{3,2,1,0:T(4,128)S(1)}, u32[]{:S(2)}, u32[]{:S(2)}) collective-permute-start(f32[1,3,4,4]{3,2,1,0:T(4,128)S(1)} %bitcast.396), channel_id=1, source_target_pairs={{0,16},{16,32},{32,48},{48,64},{64,80},{80,96},{96,112},{112,128},... | collective-permute-start | bytes 584 | tf_op jit(solution)/shard_map/ppermute | solution.py:20
  279.4 6.6 %collective-permute-start.22 = (f32[5,1,4,4]{3,2,1,0:T(4,128)S(1)}, f32[5,1,4,4]{3,2,1,0:T(4,128)S(1)}, u32[]{:S(2)}, u32[]{:S(2)}) collective-permute-start(f32[5,1,4,4]{3,2,1,0:T(4,128)S(1)} %get-tuple-element.48), channel_id=1, source_target_pairs={{0,1},{1,2},{2,3},{3,4},{4,5},{5,6},{6,7},{7,8},{8,9},{9,10},{10,1... | collective-permute-start | bytes 968 | tf_op jit(solution)/shard_map/ppermute | solution.py:20
  282.7 14.0 %collective-permute-start.23 = (f32[5,1,4,4]{3,2,1,0:T(4,128)S(1)}, f32[5,1,4,4]{3,2,1,0:T(4,128)S(1)}, u32[]{:S(2)}, u32[]{:S(2)}) collective-permute-start(f32[5,1,4,4]{3,2,1,0:T(4,128)S(1)} %get-tuple-element.47), channel_id=1, source_target_pairs={{1,0},{2,1},{3,2},{4,3},{5,4},{6,5},{7,6},{8,7},{9,8},{10,9},{11,1... | collective-permute-start | bytes 968 | tf_op jit(solution)/shard_map/ppermute | solution.py:21
  (5 other events, 5.6 us)
where the time goes:
time: 300 us; the launch traced here: 299 us
  starting transfers between devices  135 us (45%)
  waiting for transfers between devices  95.7 us (32%)
  local copies, waits for them, and re-layouts  35.5 us (12%)
  other arithmetic  21.5 us (7%)
  matrix products  8.41 us (3%)
    ppermute x12, starting transfers between devices, extended(): after = lax.ppermute(initial, axis, down)  95.8 us
    ppermute x12, waiting for transfers between devices, extended(): after = lax.ppermute(initial, axis, down)  74.4 us
    ppermute x12, starting transfers between devices, extended(): before = lax.ppermute(last, axis, up)  39.6 us
    ppermute x12, waiting for transfers between devices, extended(): before = lax.ppermute(last, axis, up)  21.3 us
    scatter-add x4, other arithmetic, local(): partial_value.at[:, centre].add(contrib).at[:, other]  9.15 us
    gather x4, local copies, waits for them, and re-layouts, local(): env_centre = env_pool[:, centre].reshape(channels, 9, count_edges)  6.51 us
    unnamed x72, local copies, waits for them, and re-layouts  6.24 us
  transfers between devices with their start and end apart: 24, of which 12 were waited for; matrix products, arithmetic and copies ran while one was open for 1% of the time, Pallas kernels for 0%

commit v1 on v0

v1 whole, which is shorter than its diff:
```python
import functools

import jax
import jax.numpy as jnp
from jax import lax
from jax.experimental import pallas as pl
from jax.experimental.pallas import tpu as pltpu
from jax.sharding import PartitionSpec as P

MESH = pl.DeviceIdType.MESH
F32 = jnp.float32
BF16 = jnp.bfloat16
OFFSETS = ((-1, -1), (-1, 0), (-1, 1), (0, -1), (0, 1), (1, -1), (1, 0), (1, 1))
AROUND = OFFSETS + ((0, 0),)
ROOT3 = 3.0 ** 0.5


def host(lx, ly):
    a, b = (72 - lx) % 64, (28 - ly) % 16
    x, zz = a // 16, a % 16
    z = zz + (x % 2) * (15 - 2 * zz)
    y, core = b // 2, b % 2
    return (z % 8) * 8 + y, x * 4 + (z // 8) * 2 + core


def column(gx, gy):
    y, x, core = gx % 8, gy // 4, gy % 2
    z = ((gy // 2) % 2) * 8 + gx // 8
    zz = z + (x % 2) * (15 - 2 * z)
    return (72 - (x * 16 + zz)) % 64, (28 - (y * 2 + core)) % 16


def iota(shape, dim):
    return lax.broadcasted_iota(jnp.int32, shape, dim)


def mm(a, b):
    return lax.dot_general(a, b, (((1,), (0,)), ((), ())), preferred_element_type=F32)


def mm_nt(a, b):
    return lax.dot_general(a, b, (((1,), (1,)), ((), ())), preferred_element_type=F32)


def top(x):
    return x.astype(BF16).astype(F32)


def split(x):
    hi = x.astype(BF16)
    return hi, (x - hi.astype(F32)).astype(BF16)


def stack3(x):
    a = top(x)
    b = top(x - a)
    return jnp.concatenate([a, b, x - a - b], axis=0).astype(BF16)


def unstack3(y, n):
    return y[:n] + y[n : 2 * n] + y[2 * n : 3 * n]


def silu(v):
    return v / (1.0 + jnp.exp(-v))


def kernel(
    nx, ny, pos_ref, spc_ref, cnt_ref, snd_ref, edg_ref, emb_c, emb_n, rad_w, env_w, lat_w, out_w, head_ref,
    energy_ref, force_ref,
    embc_v, embn_v, rad_v, env_v, lat_v, out_v,
    feat_w, expand_w, env_cat, lat_cat, sca_cat, out_cat,
    tile_near, tile_own, got_near, got_own, got_edges,
    send_part, got_part, send_env, got_env, tile_tot, got_tot,
    hid_cat, hid, pre, harm_x,
    w_sem, near_s, near_r, own_s, own_r, part_s, part_r, env_s, env_r, tot_s, tot_r,
):
    gx, gy = lax.axis_index("gx"), lax.axis_index("gy")
    lx, ly = column(gx, gy)
    beside = [((lx + dx + nx) % nx, (ly + dy + ny) % ny) for dx, dy in AROUND]
    hosts = [host(*b) for b in beside]
    targets = [host((gx + dx + nx) % nx, (gy + dy + ny) % ny) for dx, dy in AROUND]

    barrier = pltpu.get_barrier_semaphore()
    for k in range(8):
        pl.semaphore_signal(barrier, inc=1, device_id=hosts[k], device_id_type=MESH)
    for k in range(9):
        pl.semaphore_signal(barrier, inc=1, device_id=beside[k], device_id_type=MESH)

    loads = [
        pltpu.make_async_copy(src, dst, w_sem.at[i])
        for i, (src, dst) in enumerate(
            ((emb_c, embc_v), (emb_n, embn_v), (rad_w, rad_v), (env_w, env_v), (lat_w, lat_v), (out_w, out_v))
        )
    ]
    for load in loads:
        load.start()

    lane = iota((1, 128), 1)
    spread_k = ((iota((8, 128), 1) - 32) // 4 == iota((8, 128), 0)) & (iota((8, 128), 1) >= 32)
    by_lane = mm(snd_ref[0].astype(F32).astype(BF16), spread_k.astype(F32).astype(BF16))
    by_lane = jnp.where(iota((4, 128), 1) % 4 == iota((4, 128), 0), by_lane, 0.0)
    names = jnp.sum(by_lane, axis=0, keepdims=True)
    names = jnp.where(lane < 32, lane.astype(F32), jnp.where(lane < 64, names, -1.0))
    pick = (iota((32, 128), 0).astype(F32) == names).astype(F32)
    atoms = jnp.concatenate([pos_ref[...], spc_ref[...].astype(F32), jnp.zeros((4, 32), F32)], axis=0)
    picked = unstack3(mm(stack3(atoms), pick.astype(BF16)), 8)
    tile_near[...] = picked[:4]
    count_row = jnp.broadcast_to(cnt_ref[...].astype(F32), (1, 128))
    tile_own[...] = jnp.concatenate([picked[:4], names, count_row, names, names], axis=0)

    pl.semaphore_wait(barrier, 17)

    def remote(src, dst, send_sem, recv_sem, device):
        return pltpu.make_async_remote_copy(
            src_ref=src, dst_ref=dst, send_sem=send_sem, recv_sem=recv_sem, device_id=device, device_id_type=MESH
        )

    first = [
        remote(edg_ref, got_edges, own_s.at[0], own_r.at[0], targets[8]),
        remote(tile_own, got_own, own_s.at[1], own_r.at[1], targets[8]),
    ]
    first += [remote(tile_near, got_near.at[k], near_s.at[k], near_r.at[k], targets[k]) for k in range(8)]
    for copy in first:
        copy.start()

    for load in loads[:3]:
        load.wait()
    r, c, n = rad_v[...], embc_v[...], embn_v[...]
    feat_w[...] = jnp.concatenate(
        [top(r), r - top(r), top(r), top(c), c - top(c), top(n), n - top(n), jnp.zeros((72, 512), F32)], axis=0
    ).astype(BF16)
    row, col = iota((128, 640), 0), iota((128, 640), 1)
    expand_w[...] = ((row >= 64) & (row < 112) & (row % 16 == col // 64)).astype(F32).astype(BF16)
    loads[3].wait()
    for layer in range(2):
        e = 0.25 * env_v[layer]
        hi, lo = split(jnp.concatenate([e, e], axis=0).T)
        env_cat[layer, 0:512] = hi
        env_cat[layer, 512:1024] = hi
        env_cat[layer, 1024:1536] = lo
    loads[4].wait()

    def cut_latent(i, carry):
        layer, at = i // 8, pl.multiple_of((i % 8) * 64, 64)
        hi, lo = split(lat_v[layer, pl.ds(at, 64), :])
        lat_cat[layer, pl.ds(at, 64), :] = hi
        lat_cat[layer, pl.ds(pl.multiple_of(512 + at, 64), 64), :] = hi
        lat_cat[layer, pl.ds(pl.multiple_of(1024 + at, 64), 64), :] = lo
        return carry

    lax.fori_loop(0, 16, cut_latent, 0)
    for layer in range(2):
        for i, at in enumerate((576, 640, 512, 640)):
            hi, lo = split(lat_v[layer, at : at + 64, :])
            sca_cat[layer, 64 * i : 64 * i + 64] = hi
            sca_cat[layer, 256 + 64 * i : 320 + 64 * i] = hi
            sca_cat[layer, 512 + 64 * i : 576 + 64 * i] = lo
    loads[5].wait()
    for i in range(4):
        hi, lo = split(out_v[128 * i : 128 * i + 128, :].T)
        out_cat[0:512, 128 * i : 128 * i + 128] = hi
        out_cat[512:1024, 128 * i : 128 * i + 128] = hi
        out_cat[1024:1536, 128 * i : 128 * i + 128] = lo

    for copy in first:
        copy.wait_recv()

    own = got_own[...]
    pool = jnp.where(lane < 32, own[:4], 0.0)
    for k in range(8):
        pool = jnp.where((lane >= 32 + 4 * k) & (lane < 36 + 4 * k), got_near[k], pool)
    names = own[4:5]
    live = iota((1, 256), 1).astype(F32) < 8.0 * jnp.concatenate([own[5:6], own[5:6]], axis=1)
    ends = got_edges[0]
    ends = jnp.where(ends < 32, ends, 92 - ends + 2 * (ends & 3))
    ends = jnp.where(live, ends, -1)
    slot = iota((64, 256), 0)
    is_c = (slot == ends[0:1]).astype(F32)
    is_o = (slot == ends[1:2]).astype(F32)
    plus, minus = is_c + is_o, is_c - is_o
    coords = stack3(jnp.concatenate([pool, jnp.zeros((4, 128), F32)], axis=0)[:, :64])
    at_c = unstack3(mm(coords, is_c.astype(BF16)), 8)
    at_o = unstack3(mm(coords, is_o.astype(BF16)), 8)
    diff = at_o - at_c
    dx, dy, dz = diff[0:1], diff[1:2], diff[2:3]
    squared = dx * dx + dy * dy + dz * dz
    scale = 1.0 / jnp.sqrt(1.0 + squared)
    ux, uy, uz = dx * scale, dy * scale, dz * scale
    length = jnp.sqrt(squared)
    step = length - 0.5 * iota((8, 256), 0).astype(F32)
    basis = jnp.exp(-2.0 * step * step)
    kinds = iota((8, 256), 0).astype(F32)
    hot_c = (at_c[3:4] == kinds).astype(F32)
    hot_o = (at_o[3:4] == kinds).astype(F32)
    harm = jnp.concatenate(
        [
            jnp.ones_like(ux), ROOT3 * ux * uy, ROOT3 * uy * uz, 0.5 * (3.0 * uz * uz - 1.0), ROOT3 * ux * uz,
            0.5 * ROOT3 * (ux * ux - uy * uy), ux, uy, uz, jnp.zeros((7, 256), F32),
        ],
        axis=0,
    )
    h1 = top(harm)
    h2 = top(harm - h1)
    b1 = top(basis)
    feat = jnp.concatenate(
        [
            b1, b1, basis - b1, hot_c, hot_c, hot_o, hot_o, jnp.zeros((8, 256), F32),
            h1, h2, harm - h1 - h2, jnp.zeros((16, 256), F32),
        ],
        axis=0,
    ).T.astype(BF16)
    hid[...] = silu(mm(feat, feat_w[...]))
    harm_x[...] = mm(feat, expand_w[...])

    put_p = jnp.concatenate([plus, plus], axis=1).astype(BF16)
    put_m = jnp.concatenate([minus, minus], axis=1).astype(BF16)
    get_p = jnp.concatenate([plus, plus], axis=0).T.astype(BF16)
    get_m = jnp.concatenate([minus, minus], axis=0).T.astype(BF16)

    def keep_hidden():
        hi, lo = split(hid[...])
        hid_cat[:, 0:512] = hi
        hid_cat[:, 512:1024] = lo
        hid_cat[:, 1024:1536] = hi

    keep_hidden()
    same = None
    copies = []
    for layer in range(2):
        w = mm(hid_cat[...], env_cat[layer])
        contrib = jnp.concatenate([w] * 5, axis=1) * harm_x[...]
        hi, lo = split(contrib)
        both = jnp.concatenate([hi, lo], axis=0)
        part_p, part_m = mm(put_p, both[:, :384]), mm(put_m, both[:, 384:])
        part = jnp.concatenate([part_p, part_m], axis=1)
        for k in range(8):
            send_part[layer, k] = part[32 + 4 * k : 36 + 4 * k]
        back = [
            remote(
                send_part.at[layer, k], got_part.at[layer, k], part_s.at[layer, k], part_r.at[layer, k], hosts[7 - k]
            )
            for k in range(8)
        ]
        for copy in back:
            copy.start()
        copies += back
        if same is None:
            names_col = own.T[:, 4:5]
            same = (names_col[:64] == names).astype(F32)[:, :64]
            same = jnp.concatenate([same, same], axis=1).astype(BF16)
        pre[...] = mm(hid_cat[...], lat_cat[layer])
        for copy in back:
            copy.wait_recv()
        got = got_part[layer].reshape(32, 640)
        hi, lo = split(jnp.concatenate([part[:32], got], axis=0))
        env = mm(same, jnp.concatenate([hi, lo], axis=0))
        for k in range(8):
            send_env[layer, k] = env[32 + 4 * k : 36 + 4 * k]
        forth = [
            remote(send_env.at[layer, k], got_env.at[layer, k], env_s.at[layer, k], env_r.at[layer, k], hosts[k])
            for k in range(8)
        ]
        for copy in forth:
            copy.start()
        copies += forth
        for copy in forth:
            copy.wait_recv()
        got = got_env[layer].reshape(32, 640)
        hi, lo = split(jnp.concatenate([env[:32], got], axis=0))
        both = jnp.concatenate([hi, lo], axis=0)
        prod = jnp.concatenate([mm(get_p, both[:, :384]), mm(get_m, both[:, 384:])], axis=1) * harm_x[...]
        t0, t1, t2, t3, t4 = [prod[:, 128 * i : 128 * i + 128] for i in range(5)]
        t12 = t1 + t2
        low = iota((256, 128), 1) < 64
        fold = jnp.where(low, t3 + pltpu.roll(t3, 64, 1) + t4, t12 + pltpu.roll(t12, 64, 1))
        hi, lo = split(jnp.concatenate([fold, t0], axis=1))
        hid[...] += silu(pre[...] + mm(jnp.concatenate([hi, lo, hi], axis=1), sca_cat[layer]))
        keep_hidden()

    hi, lo = split(silu(mm(hid_cat[...], out_cat[...])))
    h = head_ref[...]
    hh = top(h)
    hw = jnp.concatenate([hh, h - hh, jnp.zeros((4, 512), F32)], axis=0).astype(BF16)
    by_hi, by_lo = mm_nt(hw, hi), mm_nt(hw, lo)
    heads = by_hi[0:2] + by_hi[2:4] + by_lo[0:2]
    push = heads[1:2]
    vals = jnp.concatenate([0.5 * heads[0:1], push * ux, push * uy, push * uz, jnp.zeros((4, 256), F32)], axis=0)
    vals = stack3(vals)
    tot_p, tot_m = unstack3(mm(vals, get_p), 8), unstack3(mm(vals, get_m), 8)
    tile_tot[...] = jnp.where(iota((4, 128), 0) == 0, tot_p[:4], tot_m[:4])
    last = [remote(tile_tot, got_tot.at[k], tot_s.at[k], tot_r.at[k], beside[7 - k]) for k in range(8)]
    last.append(remote(tile_tot, got_tot.at[8], tot_s.at[8], tot_r.at[8], beside[8]))
    for copy in last:
        copy.start()
    for copy in first + copies:
        copy.wait_send()
    for copy in last:
        copy.wait_recv()
    total = jnp.where(lane < 32, got_tot[8], 0.0)
    for k in range(8):
        total = jnp.where((lane >= 32 + 4 * k) & (lane < 36 + 4 * k), got_tot[k], total)
    total = stack3(jnp.concatenate([total, jnp.zeros((4, 128), F32)], axis=0))
    out = unstack3(mm_nt(total, pick.astype(BF16)), 8)
    energy_ref[...] = out[0:1]
    force_ref[...] = out[1:4]
    for copy in last:
        copy.wait_send()


def solution(mesh):
    nx, ny = mesh.shape["gx"], mesh.shape["gy"]

    def local(
        positions, species, atom_count, send_list, edges, centre_embed, neighbour_embed, radial_weight, env_weight,
        latent_weight, out_weight, head_weight,
    ):
        vmem, anywhere = pl.BlockSpec(memory_space=pltpu.VMEM), pl.BlockSpec(memory_space=pl.ANY)
        dma = pltpu.SemaphoreType.DMA
        energy, forces = pl.pallas_call(
            functools.partial(kernel, nx, ny),
            out_shape=(jax.ShapeDtypeStruct((1, 32), F32), jax.ShapeDtypeStruct((3, 32), F32)),
            in_specs=[vmem] * 5 + [anywhere] * 6 + [vmem],
            out_specs=(vmem, vmem),
            scratch_shapes=[
                pltpu.VMEM((8, 512), F32), pltpu.VMEM((8, 512), F32), pltpu.VMEM((8, 512), F32),
                pltpu.VMEM((2, 64, 512), F32), pltpu.VMEM((2, 704, 512), F32), pltpu.VMEM((512, 512), F32),
                pltpu.VMEM((128, 512), BF16), pltpu.VMEM((128, 640), BF16), pltpu.VMEM((2, 1536, 128), BF16),
                pltpu.VMEM((2, 1536, 512), BF16), pltpu.VMEM((2, 768, 512), BF16), pltpu.VMEM((1536, 512), BF16),
                pltpu.VMEM((4, 128), F32), pltpu.VMEM((8, 128), F32), pltpu.VMEM((8, 4, 128), F32),
                pltpu.VMEM((8, 128), F32), pltpu.VMEM((1, 2, 256), jnp.int32),
                pltpu.VMEM((2, 8, 4, 640), F32), pltpu.VMEM((2, 8, 4, 640), F32),
                pltpu.VMEM((2, 8, 4, 640), F32), pltpu.VMEM((2, 8, 4, 640), F32),
                pltpu.VMEM((4, 128), F32), pltpu.VMEM((9, 4, 128), F32),
                pltpu.VMEM((256, 1536), BF16), pltpu.VMEM((256, 512), F32), pltpu.VMEM((256, 512), F32),
                pltpu.VMEM((256, 640), F32),
                dma((6,)), dma((8,)), dma((8,)), dma((2,)), dma((2,)), dma((2, 8)), dma((2, 8)), dma((2, 8)),
                dma((2, 8)), dma((9,)), dma((9,)),
            ],
            compiler_params=pltpu.CompilerParams(
                collective_id=0, has_side_effects=True, vmem_limit_bytes=48 * 1024 * 1024
            ),
            name="pair_network",
        )(
            positions, species.reshape(1, -1), atom_count.reshape(1, 1), send_list.transpose(0, 2, 1), edges,
            centre_embed.T, neighbour_embed.T, radial_weight.T, env_weight, latent_weight.transpose(0, 2, 1),
            out_weight, head_weight,
        )
        return energy.reshape(-1), forces

    placed = (
        P(None, ("gx", "gy")), P(("gx", "gy")), P(("gx", "gy")), P(("gx", "gy"), None, None),
        P(("gx", "gy"), None, None), P(), P(), P(), P(), P(), P(), P(),
    )
    return jax.shard_map(
        local, mesh=mesh, in_specs=placed, out_specs=(P(("gx", "gy")), P(None, ("gx", "gy"))), check_vma=False
    )
```

time: 300 us -> 77 us (0.26)
  starting transfers between devices: 135 us -> 0 us
  waiting for transfers between devices: 95.7 us -> 0 us
  Pallas kernels: 0 us -> 63.7 us
  local copies, waits for them, and re-layouts: 35.5 us -> 10.6 us
  other arithmetic: 21.5 us -> 0 us
  matrix products: 8.41 us -> 0 us
    ppermute x24 -> x0, starting transfers between devices: 135 us -> none  [the longest x12 95.8 us: extended(): after = lax.ppermute(initial, axis, down)]
    ppermute x24 -> x0, waiting for transfers between devices: 95.7 us -> none  [the longest x12 74.4 us: extended(): after = lax.ppermute(initial, axis, down)]
    pallas_call x0 -> x1, Pallas kernels: none -> 63.7 us  [local(): pl.pallas_call(functools.partial(kernel, nx, ny), out_shape=(jax.ShapeDty...]
    scatter-add x9 -> x0, other arithmetic: 15 us -> none  [the longest x4 9.15 us: local(): partial_value.at[:, centre].add(contrib).at[:, other]]
    gather x16 -> x0, local copies, waits for them, and re-layouts: 14.3 us -> none  [the longest x4 6.51 us: local(): env_centre = env_pool[:, centre].reshape(channels, 9, count_edges)]
    reshape x20 -> x0, local copies, waits for them, and re-layouts: 9.24 us -> none  [the longest x4 5.41 us: local(): env_centre = env_pool[:, centre].reshape(channels, 9, count_edges)]
    dot_general x9 -> x0, matrix products: 8.41 us -> none  [the longest x2 3.08 us: refine(): return hidden + jax.nn.silu(jnp.dot(weight, scalars, precision=highest))]
    unnamed x72 -> x24, local copies, waits for them, and re-layouts: 6.24 us -> 10.6 us
  transfers between devices with their start and end apart: 24 -> 0, of which waited for: 12 -> 0; matrix products, arithmetic and copies ran while one was open for 1% -> 0% of each run, Pallas kernels for 0% -> 0%
where the time goes in v1:
time: 77 us; the launch traced here: 75.6 us
  Pallas kernels  63.7 us (83%)
  local copies, waits for them, and re-layouts  10.6 us (14%)
  between operations  1.31 us (2%)
    pallas_call x1, Pallas kernels, local(): pl.pallas_call(functools.partial(kernel, nx, ny), out_shape=(jax.ShapeDty...  63.7 us
    unnamed x24, local copies, waits for them, and re-layouts  10.6 us

profile of v1, /device:TPU:1, one launch (start us, length us, event | category | flops | bytes accessed | tf_op | source)
XLA Modules:
  0.0 75.6 jit_solution(1996505143188093361)
XLA Ops:
  1.3 0.0 copy-start
  1.3 1.8 %copy-done = f32[2,512,704]{1,2,0:T(8,128)S(1)} copy-done((f32[2,512,704]{1,2,0:T(8,128)S(1)}, f32[2,512,704]{1,2,0:T(8,128)}, u32[]{:S(2)}) %copy-start) | copy-done | bytes 2883608
  3.1 0.0 copy-start.1
  3.1 1.2 %copy-done.1 = f32[512,512]{1,0:T(8,128)S(1)} copy-done((f32[512,512]{1,0:T(8,128)S(1)}, f32[512,512]{1,0:T(8,128)}, u32[]{:S(2)}) %copy-start.1) | copy-done | bytes 1048600
  4.3 0.0 copy-start.2
  4.3 0.9 %copy-done.2 = f32[2,64,512]{2,1,0:T(8,128)S(1)} copy-done((f32[2,64,512]{2,1,0:T(8,128)S(1)}, f32[2,64,512]{2,1,0:T(8,128)}, u32[]{:S(2)}) %copy-start.2) | copy-done | bytes 262168
  5.3 0.0 copy-start.3
  5.3 0.7 copy-done.3
  6.0 0.0 copy-start.4
  6.0 0.7 copy-done.4
  6.7 0.0 copy-start.5
  6.7 0.7 copy-done.5
  7.4 0.0 copy-start.6
  7.4 0.7 copy-done.6
  8.1 0.0 copy-start.7
  8.1 0.7 copy-done.7
  8.8 0.0 copy-start.8
  8.8 0.7 copy-done.8
  9.5 0.0 copy-start.9
  9.5 0.7 copy-done.9
  10.2 0.0 copy-start.10
  10.2 0.7 copy-done.10
  10.8 63.7 %pair_network.1 = (f32[1,32]{1,0:T(1,128)S(1)}, f32[3,32]{1,0:T(4,128)S(1)}) custom-call(f32[3,32]{1,0:T(4,128)S(1)} %copy-done.7, s32[1,32]{1,0:T(1,128)S(1)} %bitcast.14, s32[1,1]{1,0:T(1,128)} %bitcast.8.cnt_ref, s32[1,4,8]{2,1,0:T(4,128)S(1)} %bitcast.13, s32[1,2,256]{2,1,0:T(2,128)S(1)} %copy-done.9, f32[8,512]{1,0:T(8,128)S(1)} %bitcast.10, ...), custom_call_target="tpu_custom_call" | custom-call | tf_op jit(solution)/shard_map/pair_network/pallas_call | solution.py:320
  74.6 0.5 copy.17
  75.1 0.6 copy.18
Async XLA Ops:
  1.3 1.8 %copy-start = (f32[2,512,704]{1,2,0:T(8,128)S(1)}, f32[2,512,704]{1,2,0:T(8,128)}, u32[]{:S(2)}) copy-start(f32[2,512,704]{1,2,0:T(8,128)} %param.21) | copy-start | bytes 8650756
  3.1 1.2 %copy-start.1 = (f32[512,512]{1,0:T(8,128)S(1)}, f32[512,512]{1,0:T(8,128)}, u32[]{:S(2)}) copy-start(f32[512,512]{1,0:T(8,128)} %out_w.1) | copy-start | bytes 3145732
  4.3 0.9 %copy-start.2 = (f32[2,64,512]{2,1,0:T(8,128)S(1)}, f32[2,64,512]{2,1,0:T(8,128)}, u32[]{:S(2)}) copy-start(f32[2,64,512]{2,1,0:T(8,128)} %env_w.1) | copy-start | bytes 786436
  5.3 0.7 copy-start.3
  6.0 0.7 copy-start.4
  6.7 0.7 copy-start.5
  7.4 0.7 copy-start.6
  8.1 0.7 copy-start.7
  8.8 0.7 copy-start.8
  9.5 0.7 copy-start.9
  10.2 0.7 copy-start.10

commit v2 on v1

--- a/solution.py
+++ b/solution.py
@@ -12,22 +12,26 @@
 BF16 = jnp.bfloat16
 OFFSETS = ((-1, -1), (-1, 0), (-1, 1), (0, -1), (0, 1), (1, -1), (1, 0), (1, 1))
 AROUND = OFFSETS + ((0, 0),)
+ORDER = (0, 2, 5, 7, 1, 6, 3, 4)
 ROOT3 = 3.0 ** 0.5
 
 
 def host(lx, ly):
-    a, b = (72 - lx) % 64, (28 - ly) % 16
-    x, zz = a // 16, a % 16
-    z = zz + (x % 2) * (15 - 2 * zz)
-    y, core = b // 2, b % 2
-    return (z % 8) * 8 + y, x * 4 + (z // 8) * 2 + core
+    a, b = (lx + 8) % 64, (ly + 2) % 16
+    zi, yy, t = a // 8, a % 8, b // 2
+    x = t // 2
+    z = 2 * zi + (t + x) % 2
+    y = yy + (zi % 2) * (7 - 2 * yy)
+    return (z % 8) * 8 + y, x * 4 + (z // 8) * 2 + b % 2
 
 
 def column(gx, gy):
-    y, x, core = gx % 8, gy // 4, gy % 2
+    y, x = gx % 8, gy // 4
     z = ((gy // 2) % 2) * 8 + gx // 8
-    zz = z + (x % 2) * (15 - 2 * z)
-    return (72 - (x * 16 + zz)) % 64, (28 - (y * 2 + core)) % 16
+    zi = z // 2
+    a = 8 * zi + y + (zi % 2) * (7 - 2 * y)
+    b = 4 * x + 2 * ((z + x) % 2) + gy % 2
+    return (a + 56) % 64, (b + 14) % 16
 
 
 def iota(shape, dim):
@@ -66,9 +70,9 @@
 
 
 def kernel(
-    nx, ny, pos_ref, spc_ref, cnt_ref, snd_ref, edg_ref, emb_c, emb_n, rad_w, env_w, lat_w, out_w, head_ref,
+    nx, ny, pos_h, spc_h, cnt_h, snd_h, edg_h, emb_c, emb_n, rad_w, env_w, lat_w, out_w, head_h,
     energy_ref, force_ref,
-    embc_v, embn_v, rad_v, env_v, lat_v, out_v,
+    pos_v, spc_v, cnt_v, snd_v, edg_v, embc_v, embn_v, rad_v, env_v, lat_v, out_v, head_v,
     feat_w, expand_w, env_cat, lat_cat, sca_cat, out_cat,
     tile_near, tile_own, got_near, got_own, got_edges,
     send_part, got_part, send_env, got_env, tile_tot, got_tot,
@@ -90,23 +94,28 @@
     loads = [
         pltpu.make_async_copy(src, dst, w_sem.at[i])
         for i, (src, dst) in enumerate(
-            ((emb_c, embc_v), (emb_n, embn_v), (rad_w, rad_v), (env_w, env_v), (lat_w, lat_v), (out_w, out_v))
+            (
+                (pos_h, pos_v), (spc_h, spc_v), (cnt_h, cnt_v), (snd_h, snd_v), (edg_h, edg_v), (emb_c, embc_v),
+                (emb_n, embn_v), (rad_w, rad_v), (env_w, env_v), (lat_w, lat_v), (out_w, out_v), (head_h, head_v),
+            )
         )
     ]
     for load in loads:
         load.start()
 
+    for load in loads[:5]:
+        load.wait()
     lane = iota((1, 128), 1)
     spread_k = ((iota((8, 128), 1) - 32) // 4 == iota((8, 128), 0)) & (iota((8, 128), 1) >= 32)
-    by_lane = mm(snd_ref[0].astype(F32).astype(BF16), spread_k.astype(F32).astype(BF16))
+    by_lane = mm(snd_v[0].astype(F32).astype(BF16), spread_k.astype(F32).astype(BF16))
     by_lane = jnp.where(iota((4, 128), 1) % 4 == iota((4, 128), 0), by_lane, 0.0)
     names = jnp.sum(by_lane, axis=0, keepdims=True)
     names = jnp.where(lane < 32, lane.astype(F32), jnp.where(lane < 64, names, -1.0))
     pick = (iota((32, 128), 0).astype(F32) == names).astype(F32)
-    atoms = jnp.concatenate([pos_ref[...], spc_ref[...].astype(F32), jnp.zeros((4, 32), F32)], axis=0)
+    atoms = jnp.concatenate([pos_v[...], spc_v[...].astype(F32), jnp.zeros((4, 32), F32)], axis=0)
     picked = unstack3(mm(stack3(atoms), pick.astype(BF16)), 8)
     tile_near[...] = picked[:4]
-    count_row = jnp.broadcast_to(cnt_ref[...].astype(F32), (1, 128))
+    count_row = jnp.full((1, 128), cnt_v[0], jnp.int32).astype(F32)
     tile_own[...] = jnp.concatenate([picked[:4], names, count_row, names, names], axis=0)
 
     pl.semaphore_wait(barrier, 17)
@@ -117,14 +126,14 @@
         )
 
     first = [
-        remote(edg_ref, got_edges, own_s.at[0], own_r.at[0], targets[8]),
+        remote(edg_v, got_edges, own_s.at[0], own_r.at[0], targets[8]),
         remote(tile_own, got_own, own_s.at[1], own_r.at[1], targets[8]),
     ]
     first += [remote(tile_near, got_near.at[k], near_s.at[k], near_r.at[k], targets[k]) for k in range(8)]
-    for copy in first:
-        copy.start()
-
-    for load in loads[:3]:
+    for i in (2, 4, 7, 9, 3, 8, 0, 1, 5, 6):
+        first[i].start()
+
+    for load in loads[5:8]:
         load.wait()
     r, c, n = rad_v[...], embc_v[...], embn_v[...]
     feat_w[...] = jnp.concatenate(
@@ -132,14 +141,14 @@
     ).astype(BF16)
     row, col = iota((128, 640), 0), iota((128, 640), 1)
     expand_w[...] = ((row >= 64) & (row < 112) & (row % 16 == col // 64)).astype(F32).astype(BF16)
-    loads[3].wait()
+    loads[8].wait()
     for layer in range(2):
         e = 0.25 * env_v[layer]
         hi, lo = split(jnp.concatenate([e, e], axis=0).T)
         env_cat[layer, 0:512] = hi
         env_cat[layer, 512:1024] = hi
         env_cat[layer, 1024:1536] = lo
-    loads[4].wait()
+    loads[9].wait()
 
     def cut_latent(i, carry):
         layer, at = i // 8, pl.multiple_of((i % 8) * 64, 64)
@@ -156,7 +165,7 @@
             sca_cat[layer, 64 * i : 64 * i + 64] = hi
             sca_cat[layer, 256 + 64 * i : 320 + 64 * i] = hi
             sca_cat[layer, 512 + 64 * i : 576 + 64 * i] = lo
-    loads[5].wait()
+    loads[10].wait()
     for i in range(4):
         hi, lo = split(out_v[128 * i : 128 * i + 128, :].T)
         out_cat[0:512, 128 * i : 128 * i + 128] = hi
@@ -242,8 +251,8 @@
             )
             for k in range(8)
         ]
-        for copy in back:
-            copy.start()
+        for k in ORDER:
+            back[k].start()
         copies += back
         if same is None:
             names_col = own.T[:, 4:5]
@@ -261,8 +270,8 @@
             remote(send_env.at[layer, k], got_env.at[layer, k], env_s.at[layer, k], env_r.at[layer, k], hosts[k])
             for k in range(8)
         ]
-        for copy in forth:
-            copy.start()
+        for k in ORDER:
+            forth[k].start()
         copies += forth
         for copy in forth:
             copy.wait_recv()
@@ -279,7 +288,8 @@
         keep_hidden()
 
     hi, lo = split(silu(mm(hid_cat[...], out_cat[...])))
-    h = head_ref[...]
+    loads[11].wait()
+    h = head_v[...]
     hh = top(h)
     hw = jnp.concatenate([hh, h - hh, jnp.zeros((4, 512), F32)], axis=0).astype(BF16)
     by_hi, by_lo = mm_nt(hw, hi), mm_nt(hw, lo)
@@ -320,12 +330,14 @@
         energy, forces = pl.pallas_call(
             functools.partial(kernel, nx, ny),
             out_shape=(jax.ShapeDtypeStruct((1, 32), F32), jax.ShapeDtypeStruct((3, 32), F32)),
-            in_specs=[vmem] * 5 + [anywhere] * 6 + [vmem],
+            in_specs=[anywhere] * 12,
             out_specs=(vmem, vmem),
             scratch_shapes=[
+                pltpu.VMEM((3, 32), F32), pltpu.VMEM((1, 32), jnp.int32), pltpu.SMEM((1,), jnp.int32),
+                pltpu.VMEM((1, 4, 8), jnp.int32), pltpu.VMEM((1, 2, 256), jnp.int32),
                 pltpu.VMEM((8, 512), F32), pltpu.VMEM((8, 512), F32), pltpu.VMEM((8, 512), F32),
                 pltpu.VMEM((2, 64, 512), F32), pltpu.VMEM((2, 704, 512), F32), pltpu.VMEM((512, 512), F32),
-                pltpu.VMEM((128, 512), BF16), pltpu.VMEM((128, 640), BF16), pltpu.VMEM((2, 1536, 128), BF16),
+                pltpu.VMEM((2, 512), F32), pltpu.VMEM((128, 512), BF16), pltpu.VMEM((128, 640), BF16), pltpu.VMEM((2, 1536, 128), BF16),
                 pltpu.VMEM((2, 1536, 512), BF16), pltpu.VMEM((2, 768, 512), BF16), pltpu.VMEM((1536, 512), BF16),
                 pltpu.VMEM((4, 128), F32), pltpu.VMEM((8, 128), F32), pltpu.VMEM((8, 4, 128), F32),
                 pltpu.VMEM((8, 128), F32), pltpu.VMEM((1, 2, 256), jnp.int32),
@@ -334,15 +346,15 @@
                 pltpu.VMEM((4, 128), F32), pltpu.VMEM((9, 4, 128), F32),
                 pltpu.VMEM((256, 1536), BF16), pltpu.VMEM((256, 512), F32), pltpu.VMEM((256, 512), F32),
                 pltpu.VMEM((256, 640), F32),
-                dma((6,)), dma((8,)), dma((8,)), dma((2,)), dma((2,)), dma((2, 8)), dma((2, 8)), dma((2, 8)),
+                dma((12,)), dma((8,)), dma((8,)), dma((2,)), dma((2,)), dma((2, 8)), dma((2, 8)), dma((2, 8)),
                 dma((2, 8)), dma((9,)), dma((9,)),
             ],
             compiler_params=pltpu.CompilerParams(
-                collective_id=0, has_side_effects=True, vmem_limit_bytes=48 * 1024 * 1024
+                collective_id=0, has_side_effects=True, vmem_limit_bytes=64 * 1024 * 1024
             ),
             name="pair_network",
         )(
-            positions, species.reshape(1, -1), atom_count.reshape(1, 1), send_list.transpose(0, 2, 1), edges,
+            positions, species.reshape(1, -1), atom_count, send_list.transpose(0, 2, 1), edges,
             centre_embed.T, neighbour_embed.T, radial_weight.T, env_weight, latent_weight.transpose(0, 2, 1),
             out_weight, head_weight,
         )

time: 77 us -> 62.2 us (0.81); the launches traced: 75.6 us -> 62 us
  local copies, waits for them, and re-layouts: 10.6 us -> 2.39 us
  Pallas kernels: 63.7 us -> 58.3 us
    unnamed x24 -> x2, local copies, waits for them, and re-layouts: 10.6 us -> 2.39 us
    pallas_call x1, Pallas kernels: 63.7 us -> 58.3 us  [local(): pl.pallas_call(functools.partial(kernel, nx, ny), out_shape=(jax.ShapeDty...]
where the time goes in v2:
time: 62.2 us; the launch traced here: 62 us
  Pallas kernels  58.3 us (94%)
  local copies, waits for them, and re-layouts  2.39 us (4%)
  between operations  1.29 us (2%)
    pallas_call x1, Pallas kernels, local(): pl.pallas_call(functools.partial(kernel, nx, ny), out_shape=(jax.ShapeDty...  58.3 us
    unnamed x2, local copies, waits for them, and re-layouts  2.39 us

profile of v2, /device:TPU:1, one launch (start us, length us, event | category | flops | bytes accessed | tf_op | source)
XLA Modules:
  0.0 62.0 jit_solution(5126612912650788198)
XLA Ops:
  1.3 58.3 %pair_network.1 = (f32[1,32]{1,0:T(1,128)}, f32[3,32]{1,0:T(4,128)}) custom-call(f32[3,32]{1,0:T(4,128)} %pos_h.1, s32[1,32]{1,0:T(1,128)} %bitcast.12, s32[1]{0:T(128)S(6)} %copy.16.cnt_h, s32[1,4,8]{2,1,0:T(4,128)} %bitcast.11, s32[1,2,256]{2,1,0:T(2,128)} %edg_h.1, f32[8,512]{1,0:T(8,128)} %bitcast.8, f32[8,512]{1,0:T(8,128)} %bitcast.9, ...), custom_call_target="tpu_custom_call" | custom-call | tf_op jit(solution)/shard_map/pair_network/pallas_call | solution.py:330
  59.6 1.1 %copy.17 = f32[32]{0:T(128)} copy(f32[32]{0:T(128)} %bitcast.13) | data formatting | bytes 256
  60.7 1.2 %copy.18 = f32[3,32]{1,0:T(4,128)} copy(f32[3,32]{1,0:T(4,128)} %get-tuple-element.9) | data formatting | bytes 768

commit v3 on v2

--- a/solution.py
+++ b/solution.py
@@ -69,15 +69,25 @@
     return v / (1.0 + jnp.exp(-v))
 
 
+def picked_names(snd_v):
+    lane = iota((1, 128), 1)
+    spread_k = ((iota((8, 128), 1) - 32) // 4 == iota((8, 128), 0)) & (iota((8, 128), 1) >= 32)
+    by_lane = mm(snd_v[0].astype(F32).astype(BF16), spread_k.astype(F32).astype(BF16))
+    by_lane = jnp.where(iota((4, 128), 1) % 4 == iota((4, 128), 0), by_lane, 0.0)
+    names = jnp.sum(by_lane, axis=0, keepdims=True)
+    names = jnp.where(lane < 32, lane.astype(F32), jnp.where(lane < 64, names, -1.0))
+    return names
+
+
 def kernel(
     nx, ny, pos_h, spc_h, cnt_h, snd_h, edg_h, emb_c, emb_n, rad_w, env_w, lat_w, out_w, head_h,
-    energy_ref, force_ref,
+    got_tot, names_h,
     pos_v, spc_v, cnt_v, snd_v, edg_v, embc_v, embn_v, rad_v, env_v, lat_v, out_v, head_v,
     feat_w, expand_w, env_cat, lat_cat, sca_cat, out_cat,
     tile_near, tile_own, got_near, got_own, got_edges,
-    send_part, got_part, send_env, got_env, tile_tot, got_tot,
+    send_part, got_part, send_env, got_env, tile_tot,
     hid_cat, hid, pre, harm_x,
-    w_sem, near_s, near_r, own_s, own_r, part_s, part_r, env_s, env_r, tot_s, tot_r,
+    w_sem, near_s, near_r, own_s, own_r, part_s, part_r, env_s, env_r, tot_s, tot_r, name_sem,
 ):
     gx, gy = lax.axis_index("gx"), lax.axis_index("gy")
     lx, ly = column(gx, gy)
@@ -86,9 +96,7 @@
     targets = [host((gx + dx + nx) % nx, (gy + dy + ny) % ny) for dx, dy in AROUND]
 
     barrier = pltpu.get_barrier_semaphore()
-    for k in range(8):
-        pl.semaphore_signal(barrier, inc=1, device_id=hosts[k], device_id_type=MESH)
-    for k in range(9):
+    for k in (0, 2, 5, 7, 1, 6, 3, 4, 8):
         pl.semaphore_signal(barrier, inc=1, device_id=beside[k], device_id_type=MESH)
 
     loads = [
@@ -106,19 +114,17 @@
     for load in loads[:5]:
         load.wait()
     lane = iota((1, 128), 1)
-    spread_k = ((iota((8, 128), 1) - 32) // 4 == iota((8, 128), 0)) & (iota((8, 128), 1) >= 32)
-    by_lane = mm(snd_v[0].astype(F32).astype(BF16), spread_k.astype(F32).astype(BF16))
-    by_lane = jnp.where(iota((4, 128), 1) % 4 == iota((4, 128), 0), by_lane, 0.0)
-    names = jnp.sum(by_lane, axis=0, keepdims=True)
-    names = jnp.where(lane < 32, lane.astype(F32), jnp.where(lane < 64, names, -1.0))
+    names = picked_names(snd_v)
     pick = (iota((32, 128), 0).astype(F32) == names).astype(F32)
     atoms = jnp.concatenate([pos_v[...], spc_v[...].astype(F32), jnp.zeros((4, 32), F32)], axis=0)
     picked = unstack3(mm(stack3(atoms), pick.astype(BF16)), 8)
     tile_near[...] = picked[:4]
     count_row = jnp.full((1, 128), cnt_v[0], jnp.int32).astype(F32)
     tile_own[...] = jnp.concatenate([picked[:4], names, count_row, names, names], axis=0)
-
-    pl.semaphore_wait(barrier, 17)
+    keep_names = pltpu.make_async_copy(tile_own, names_h, name_sem.at[0])
+    keep_names.start()
+
+    pl.semaphore_wait(barrier, 9)
 
     def remote(src, dst, send_sem, recv_sem, device):
         return pltpu.make_async_remote_copy(
@@ -224,8 +230,6 @@
 
     put_p = jnp.concatenate([plus, plus], axis=1).astype(BF16)
     put_m = jnp.concatenate([minus, minus], axis=1).astype(BF16)
-    get_p = jnp.concatenate([plus, plus], axis=0).T.astype(BF16)
-    get_m = jnp.concatenate([minus, minus], axis=0).T.astype(BF16)
 
     def keep_hidden():
         hi, lo = split(hid[...])
@@ -258,6 +262,8 @@
             names_col = own.T[:, 4:5]
             same = (names_col[:64] == names).astype(F32)[:, :64]
             same = jnp.concatenate([same, same], axis=1).astype(BF16)
+            get_p = jnp.concatenate([plus, plus], axis=0).T.astype(BF16)
+            get_m = jnp.concatenate([minus, minus], axis=0).T.astype(BF16)
         pre[...] = mm(hid_cat[...], lat_cat[layer])
         for copy in back:
             copy.wait_recv()
@@ -305,17 +311,33 @@
         copy.start()
     for copy in first + copies:
         copy.wait_send()
+    keep_names.wait()
     for copy in last:
         copy.wait_recv()
-    total = jnp.where(lane < 32, got_tot[8], 0.0)
+    for copy in last:
+        copy.wait_send()
+
+
+def owner_kernel(tot_h, names_h, energy_h, force_h, tot_v, names_v, energy_v, force_v, sem):
+    loads = [pltpu.make_async_copy(tot_h, tot_v, sem.at[0]), pltpu.make_async_copy(names_h, names_v, sem.at[1])]
+    for load in loads:
+        load.start()
+    for load in loads:
+        load.wait()
+    lane = iota((1, 128), 1)
+    pick = (iota((32, 128), 0).astype(F32) == names_v[4:5]).astype(F32)
+    total = jnp.where(lane < 32, tot_v[8], 0.0)
     for k in range(8):
-        total = jnp.where((lane >= 32 + 4 * k) & (lane < 36 + 4 * k), got_tot[k], total)
+        total = jnp.where((lane >= 32 + 4 * k) & (lane < 36 + 4 * k), tot_v[k], total)
     total = stack3(jnp.concatenate([total, jnp.zeros((4, 128), F32)], axis=0))
     out = unstack3(mm_nt(total, pick.astype(BF16)), 8)
-    energy_ref[...] = out[0:1]
-    force_ref[...] = out[1:4]
-    for copy in last:
-        copy.wait_send()
+    energy_v[...] = out[0:1]
+    force_v[...] = out[1:4]
+    stores = [pltpu.make_async_copy(energy_v, energy_h, sem.at[2]), pltpu.make_async_copy(force_v, force_h, sem.at[3])]
+    for store in stores:
+        store.start()
+    for store in stores:
+        store.wait()
 
 
 def solution(mesh):
@@ -325,13 +347,13 @@
         positions, species, atom_count, send_list, edges, centre_embed, neighbour_embed, radial_weight, env_weight,
         latent_weight, out_weight, head_weight,
     ):
-        vmem, anywhere = pl.BlockSpec(memory_space=pltpu.VMEM), pl.BlockSpec(memory_space=pl.ANY)
+        anywhere = pl.BlockSpec(memory_space=pl.ANY)
         dma = pltpu.SemaphoreType.DMA
-        energy, forces = pl.pallas_call(
+        totals, names = pl.pallas_call(
             functools.partial(kernel, nx, ny),
-            out_shape=(jax.ShapeDtypeStruct((1, 32), F32), jax.ShapeDtypeStruct((3, 32), F32)),
+            out_shape=(jax.ShapeDtypeStruct((9, 4, 128), F32), jax.ShapeDtypeStruct((8, 128), F32)),
             in_specs=[anywhere] * 12,
-            out_specs=(vmem, vmem),
+            out_specs=(anywhere, anywhere),
             scratch_shapes=[
                 pltpu.VMEM((3, 32), F32), pltpu.VMEM((1, 32), jnp.int32), pltpu.SMEM((1,), jnp.int32),
                 pltpu.VMEM((1, 4, 8), jnp.int32), pltpu.VMEM((1, 2, 256), jnp.int32),
@@ -343,11 +365,11 @@
                 pltpu.VMEM((8, 128), F32), pltpu.VMEM((1, 2, 256), jnp.int32),
                 pltpu.VMEM((2, 8, 4, 640), F32), pltpu.VMEM((2, 8, 4, 640), F32),
                 pltpu.VMEM((2, 8, 4, 640), F32), pltpu.VMEM((2, 8, 4, 640), F32),
-                pltpu.VMEM((4, 128), F32), pltpu.VMEM((9, 4, 128), F32),
+                pltpu.VMEM((4, 128), F32),
                 pltpu.VMEM((256, 1536), BF16), pltpu.VMEM((256, 512), F32), pltpu.VMEM((256, 512), F32),
                 pltpu.VMEM((256, 640), F32),
                 dma((12,)), dma((8,)), dma((8,)), dma((2,)), dma((2,)), dma((2, 8)), dma((2, 8)), dma((2, 8)),
-                dma((2, 8)), dma((9,)), dma((9,)),
+                dma((2, 8)), dma((9,)), dma((9,)), dma((1,)),
             ],
             compiler_params=pltpu.CompilerParams(
                 collective_id=0, has_side_effects=True, vmem_limit_bytes=64 * 1024 * 1024
@@ -358,6 +380,18 @@
             centre_embed.T, neighbour_embed.T, radial_weight.T, env_weight, latent_weight.transpose(0, 2, 1),
             out_weight, head_weight,
         )
+        energy, forces = pl.pallas_call(
+            owner_kernel,
+            out_shape=(jax.ShapeDtypeStruct((1, 32), F32), jax.ShapeDtypeStruct((3, 32), F32)),
+            in_specs=[anywhere] * 2,
+            out_specs=(anywhere, anywhere),
+            scratch_shapes=[
+                pltpu.VMEM((9, 4, 128), F32), pltpu.VMEM((8, 128), F32), pltpu.VMEM((1, 32), F32),
+                pltpu.VMEM((3, 32), F32), dma((4,)),
+            ],
+            compiler_params=pltpu.CompilerParams(vmem_limit_bytes=64 * 1024 * 1024),
+            name="owner_sums",
+        )(totals, names)
         return energy.reshape(-1), forces
 
     placed = (

time: 62.2 us -> 60.6 us (0.974)
  local copies, waits for them, and re-layouts: 2.39 us -> 0 us
  Pallas kernels: 58.3 us -> 59 us
    unnamed x2 -> x0, local copies, waits for them, and re-layouts: 2.39 us -> none
    pallas_call x0 -> x1, Pallas kernels: none -> 1.46 us  [local(): pl.pallas_call(owner_kernel, out_shape=(jax.ShapeDtypeStruct((1, 32), F32...]
    pallas_call x1, Pallas kernels: 58.3 us -> 57.6 us  [local(): pl.pallas_call(functools.partial(kernel, nx, ny), out_shape=(jax.ShapeDty...]
where the time goes in v3:
time: 60.6 us; the launch traced here: 60.3 us
  Pallas kernels  59 us (97%)
  between operations  1.29 us (2%)
    pallas_call x1, Pallas kernels, local(): pl.pallas_call(functools.partial(kernel, nx, ny), out_shape=(jax.ShapeDty...  57.6 us
    pallas_call x1, Pallas kernels, local(): pl.pallas_call(owner_kernel, out_shape=(jax.ShapeDtypeStruct((1, 32), F32...  1.46 us

profile of v3, /device:TPU:1, one launch (start us, length us, event | category | flops | bytes accessed | tf_op | source)
XLA Modules:
  0.0 60.3 jit_solution(16712951663611640446)
XLA Ops:
  1.3 57.6 %pair_network.1 = (f32[9,4,128]{2,1,0:T(4,128)}, f32[8,128]{1,0:T(8,128)}) custom-call(f32[3,32]{1,0:T(4,128)} %pos_h.1, s32[1,32]{1,0:T(1,128)} %bitcast.12, s32[1]{0:T(128)S(6)} %copy.14.cnt_h, s32[1,4,8]{2,1,0:T(4,128)} %bitcast.11, s32[1,2,256]{2,1,0:T(2,128)} %edg_h.1, f32[8,512]{1,0:T(8,128)} %bitcast.8, f32[8,512]{1,0:T(8,128)} %bitcast.9, ...), custom_call_target="tpu_custom_call" | custom-call | tf_op jit(solution)/shard_map/pair_network/pallas_call | solution.py:352
  58.8 1.5 %owner_sums.1 = (f32[1,32]{1,0:T(1,128)}, f32[3,32]{1,0:T(4,128)}) custom-call(f32[9,4,128]{2,1,0:T(4,128)} %get-tuple-element.6.tot_h, f32[8,128]{1,0:T(8,128)} %get-tuple-element.7.names_h), custom_call_target="tpu_custom_call" | custom-call | tf_op jit(solution)/shard_map/owner_sums/pallas_call | solution.py:383

commit v4 on v3

--- a/solution.py
+++ b/solution.py
@@ -17,21 +17,21 @@
 
 
 def host(lx, ly):
-    a, b = (lx + 8) % 64, (ly + 2) % 16
+    a, b = (lx + 46) % 64, (ly + 2) % 16
     zi, yy, t = a // 8, a % 8, b // 2
     x = t // 2
-    z = 2 * zi + (t + x) % 2
-    y = yy + (zi % 2) * (7 - 2 * yy)
+    z = (2 * zi + (t + x) % 2 + 6) % 16
+    y = (yy + (zi % 2) * (7 - 2 * yy) + 3) % 8
     return (z % 8) * 8 + y, x * 4 + (z // 8) * 2 + b % 2
 
 
 def column(gx, gy):
-    y, x = gx % 8, gy // 4
-    z = ((gy // 2) % 2) * 8 + gx // 8
+    y, x = (gx % 8 + 5) % 8, gy // 4
+    z = (((gy // 2) % 2) * 8 + gx // 8 + 10) % 16
     zi = z // 2
     a = 8 * zi + y + (zi % 2) * (7 - 2 * y)
     b = 4 * x + 2 * ((z + x) % 2) + gy % 2
-    return (a + 56) % 64, (b + 14) % 16
+    return (a + 18) % 64, (b + 14) % 16
 
 
 def iota(shape, dim):
@@ -95,10 +95,6 @@
     hosts = [host(*b) for b in beside]
     targets = [host((gx + dx + nx) % nx, (gy + dy + ny) % ny) for dx, dy in AROUND]
 
-    barrier = pltpu.get_barrier_semaphore()
-    for k in (0, 2, 5, 7, 1, 6, 3, 4, 8):
-        pl.semaphore_signal(barrier, inc=1, device_id=beside[k], device_id_type=MESH)
-
     loads = [
         pltpu.make_async_copy(src, dst, w_sem.at[i])
         for i, (src, dst) in enumerate(
@@ -108,7 +104,13 @@
             )
         )
     ]
-    for load in loads:
+    for load in loads[:5]:
+        load.start()
+
+    barrier = pltpu.get_barrier_semaphore()
+    for k in (0, 2, 5, 7, 1, 6, 3, 4, 8):
+        pl.semaphore_signal(barrier, inc=1, device_id=beside[k], device_id_type=MESH)
+    for load in loads[5:]:
         load.start()
 
     for load in loads[:5]:
@@ -322,10 +324,10 @@
     loads = [pltpu.make_async_copy(tot_h, tot_v, sem.at[0]), pltpu.make_async_copy(names_h, names_v, sem.at[1])]
     for load in loads:
         load.start()
-    for load in loads:
-        load.wait()
     lane = iota((1, 128), 1)
+    loads[1].wait()
     pick = (iota((32, 128), 0).astype(F32) == names_v[4:5]).astype(F32)
+    loads[0].wait()
     total = jnp.where(lane < 32, tot_v[8], 0.0)
     for k in range(8):
         total = jnp.where((lane >= 32 + 4 * k) & (lane < 36 + 4 * k), tot_v[k], total)

time: 60.6 us -> 58.8 us (0.970)
  the two profiles are of different devices: /device:TPU:1 before, /device:TPU:391 now
where the time goes in v4:
time: 58.8 us; the launch traced here: 58.6 us
  Pallas kernels  57.3 us (97%)
  between operations  1.29 us (2%)
    pallas_call x1, Pallas kernels, local(): pl.pallas_call(functools.partial(kernel, nx, ny), out_shape=(jax.ShapeDty...  55.8 us
    pallas_call x1, Pallas kernels, local(): pl.pallas_call(owner_kernel, out_shape=(jax.ShapeDtypeStruct((1, 32), F32...  1.46 us

profile of v4, /device:TPU:391, one launch (start us, length us, event | category | flops | bytes accessed | tf_op | source)
XLA Modules:
  0.0 58.6 jit_solution(15007699161259422035)
XLA Ops:
  1.3 55.8 %pair_network.1 = (f32[9,4,128]{2,1,0:T(4,128)}, f32[8,128]{1,0:T(8,128)}) custom-call(f32[3,32]{1,0:T(4,128)} %pos_h.1, s32[1,32]{1,0:T(1,128)} %bitcast.12, s32[1]{0:T(128)S(6)} %copy.14.cnt_h, s32[1,4,8]{2,1,0:T(4,128)} %bitcast.11, s32[1,2,256]{2,1,0:T(2,128)} %edg_h.1, f32[8,512]{1,0:T(8,128)} %bitcast.8, f32[8,512]{1,0:T(8,128)} %bitcast.9, ...), custom_call_target="tpu_custom_call" | custom-call | tf_op jit(solution)/shard_map/pair_network/pallas_call | solution.py:354
  57.1 1.5 %owner_sums.1 = (f32[1,32]{1,0:T(1,128)}, f32[3,32]{1,0:T(4,128)}) custom-call(f32[9,4,128]{2,1,0:T(4,128)} %get-tuple-element.6.tot_h, f32[8,128]{1,0:T(8,128)} %get-tuple-element.7.names_h), custom_call_target="tpu_custom_call" | custom-call | tf_op jit(solution)/shard_map/owner_sums/pallas_call | solution.py:385

commit v5 on v4

--- a/solution.py
+++ b/solution.py
@@ -16,22 +16,30 @@
 ROOT3 = 3.0 ** 0.5
 
 
+def div(a, b):
+    return lax.div(a, jnp.int32(b))
+
+
+def rem(a, b):
+    return lax.rem(a, jnp.int32(b))
+
+
 def host(lx, ly):
-    a, b = (lx + 46) % 64, (ly + 2) % 16
-    zi, yy, t = a // 8, a % 8, b // 2
-    x = t // 2
-    z = (2 * zi + (t + x) % 2 + 6) % 16
-    y = (yy + (zi % 2) * (7 - 2 * yy) + 3) % 8
-    return (z % 8) * 8 + y, x * 4 + (z // 8) * 2 + b % 2
+    a, b = rem(lx + 46, 64), rem(ly + 2, 16)
+    zi, yy, t = div(a, 8), rem(a, 8), div(b, 2)
+    x = div(t, 2)
+    z = rem(2 * zi + rem(t + x, 2) + 6, 16)
+    y = rem(yy + rem(zi, 2) * (7 - 2 * yy) + 3, 8)
+    return rem(z, 8) * 8 + y, x * 4 + div(z, 8) * 2 + rem(b, 2)
 
 
 def column(gx, gy):
-    y, x = (gx % 8 + 5) % 8, gy // 4
-    z = (((gy // 2) % 2) * 8 + gx // 8 + 10) % 16
-    zi = z // 2
-    a = 8 * zi + y + (zi % 2) * (7 - 2 * y)
-    b = 4 * x + 2 * ((z + x) % 2) + gy % 2
-    return (a + 18) % 64, (b + 14) % 16
+    y, x = rem(rem(gx, 8) + 5, 8), div(gy, 4)
+    z = rem(rem(div(gy, 2), 2) * 8 + div(gx, 8) + 10, 16)
+    zi = div(z, 2)
+    a = 8 * zi + y + rem(zi, 2) * (7 - 2 * y)
+    b = 4 * x + 2 * rem(z + x, 2) + rem(gy, 2)
+    return rem(a + 18, 64), rem(b + 14, 16)
 
 
 def iota(shape, dim):
@@ -91,9 +99,7 @@
 ):
     gx, gy = lax.axis_index("gx"), lax.axis_index("gy")
     lx, ly = column(gx, gy)
-    beside = [((lx + dx + nx) % nx, (ly + dy + ny) % ny) for dx, dy in AROUND]
-    hosts = [host(*b) for b in beside]
-    targets = [host((gx + dx + nx) % nx, (gy + dy + ny) % ny) for dx, dy in AROUND]
+    beside = [(rem(lx + dx + nx, nx), rem(ly + dy + ny, ny)) for dx, dy in AROUND]
 
     loads = [
         pltpu.make_async_copy(src, dst, w_sem.at[i])
@@ -112,6 +118,8 @@
         pl.semaphore_signal(barrier, inc=1, device_id=beside[k], device_id_type=MESH)
     for load in loads[5:]:
         load.start()
+
+    targets = [host(rem(gx + dx + nx, nx), rem(gy + dy + ny, ny)) for dx, dy in AROUND]
 
     for load in loads[:5]:
         load.wait()
@@ -140,6 +148,8 @@
     first += [remote(tile_near, got_near.at[k], near_s.at[k], near_r.at[k], targets[k]) for k in range(8)]
     for i in (2, 4, 7, 9, 3, 8, 0, 1, 5, 6):
         first[i].start()
+
+    hosts = [host(*b) for b in beside]
 
     for load in loads[5:8]:
         load.wait()

time: 58.8 us -> 58.4 us (level)
  no operation moved by 1% of the time
where the time goes in v5:
time: 58.4 us; the launch traced here: 58.2 us
  Pallas kernels  56.9 us (97%)
  between operations  1.29 us (2%)
    pallas_call x1, Pallas kernels, local(): pl.pallas_call(functools.partial(kernel, nx, ny), out_shape=(jax.ShapeDty...  55.4 us
    pallas_call x1, Pallas kernels, local(): pl.pallas_call(owner_kernel, out_shape=(jax.ShapeDtypeStruct((1, 32), F32...  1.46 us

profile of v5, /device:TPU:391, one launch (start us, length us, event | category | flops | bytes accessed | tf_op | source)
XLA Modules:
  0.0 58.2 jit_solution(11185089544309510935)
XLA Ops:
  1.3 55.4 %pair_network.1 = (f32[9,4,128]{2,1,0:T(4,128)}, f32[8,128]{1,0:T(8,128)}) custom-call(f32[3,32]{1,0:T(4,128)} %pos_h.1, s32[1,32]{1,0:T(1,128)} %bitcast.12, s32[1]{0:T(128)S(6)} %copy.14.cnt_h, s32[1,4,8]{2,1,0:T(4,128)} %bitcast.11, s32[1,2,256]{2,1,0:T(2,128)} %edg_h.1, f32[8,512]{1,0:T(8,128)} %bitcast.8, f32[8,512]{1,0:T(8,128)} %bitcast.9, ...), custom_call_target="tpu_custom_call" | custom-call | tf_op jit(solution)/shard_map/pair_network/pallas_call | solution.py:364
  56.7 1.5 %owner_sums.1 = (f32[1,32]{1,0:T(1,128)}, f32[3,32]{1,0:T(4,128)}) custom-call(f32[9,4,128]{2,1,0:T(4,128)} %get-tuple-element.6.tot_h, f32[8,128]{1,0:T(8,128)} %get-tuple-element.7.names_h), custom_call_target="tpu_custom_call" | custom-call | tf_op jit(solution)/shard_map/owner_sums/pallas_call | solution.py:395

commit v6 on v5

--- a/solution.py
+++ b/solution.py
@@ -259,8 +259,6 @@
         both = jnp.concatenate([hi, lo], axis=0)
         part_p, part_m = mm(put_p, both[:, :384]), mm(put_m, both[:, 384:])
         part = jnp.concatenate([part_p, part_m], axis=1)
-        for k in range(8):
-            send_part[layer, k] = part[32 + 4 * k : 36 + 4 * k]
         back = [
             remote(
                 send_part.at[layer, k], got_part.at[layer, k], part_s.at[layer, k], part_r.at[layer, k], hosts[7 - k]
@@ -268,6 +266,7 @@
             for k in range(8)
         ]
         for k in ORDER:
+            send_part[layer, k] = part[32 + 4 * k : 36 + 4 * k]
             back[k].start()
         copies += back
         if same is None:
@@ -281,20 +280,21 @@
             copy.wait_recv()
         got = got_part[layer].reshape(32, 640)
         hi, lo = split(jnp.concatenate([part[:32], got], axis=0))
-        env = mm(same, jnp.concatenate([hi, lo], axis=0))
-        for k in range(8):
-            send_env[layer, k] = env[32 + 4 * k : 36 + 4 * k]
+        both = jnp.concatenate([hi, lo], axis=0)
+        picks = mm(same[32:], both)
         forth = [
             remote(send_env.at[layer, k], got_env.at[layer, k], env_s.at[layer, k], env_r.at[layer, k], hosts[k])
             for k in range(8)
         ]
         for k in ORDER:
+            send_env[layer, k] = picks[4 * k : 4 * k + 4]
             forth[k].start()
+        env = mm(same[:32], both)
         copies += forth
         for copy in forth:
             copy.wait_recv()
         got = got_env[layer].reshape(32, 640)
-        hi, lo = split(jnp.concatenate([env[:32], got], axis=0))
+        hi, lo = split(jnp.concatenate([env, got], axis=0))
         both = jnp.concatenate([hi, lo], axis=0)
         prod = jnp.concatenate([mm(get_p, both[:, :384]), mm(get_m, both[:, 384:])], axis=1) * harm_x[...]
         t0, t1, t2, t3, t4 = [prod[:, 128 * i : 128 * i + 128] for i in range(5)]

time: 58.4 us -> 58.5 us (level)
  no operation moved by 1% of the time
where the time goes in v6:
time: 58.5 us; the launch traced here: 58.3 us
  Pallas kernels  57 us (97%)
  between operations  1.29 us (2%)
    pallas_call x1, Pallas kernels, local(): pl.pallas_call(functools.partial(kernel, nx, ny), out_shape=(jax.ShapeDty...  55.5 us
    pallas_call x1, Pallas kernels, local(): pl.pallas_call(owner_kernel, out_shape=(jax.ShapeDtypeStruct((1, 32), F32...  1.46 us

profile of v6, /device:TPU:391, one launch (start us, length us, event | category | flops | bytes accessed | tf_op | source)
XLA Modules:
  0.0 58.3 jit_solution(7635397350464213149)
XLA Ops:
  1.3 55.5 %pair_network.1 = (f32[9,4,128]{2,1,0:T(4,128)}, f32[8,128]{1,0:T(8,128)}) custom-call(f32[3,32]{1,0:T(4,128)} %pos_h.1, s32[1,32]{1,0:T(1,128)} %bitcast.12, s32[1]{0:T(128)S(6)} %copy.14.cnt_h, s32[1,4,8]{2,1,0:T(4,128)} %bitcast.11, s32[1,2,256]{2,1,0:T(2,128)} %edg_h.1, f32[8,512]{1,0:T(8,128)} %bitcast.8, f32[8,512]{1,0:T(8,128)} %bitcast.9, ...), custom_call_target="tpu_custom_call" | custom-call | tf_op jit(solution)/shard_map/pair_network/pallas_call | solution.py:364
  56.8 1.5 %owner_sums.1 = (f32[1,32]{1,0:T(1,128)}, f32[3,32]{1,0:T(4,128)}) custom-call(f32[9,4,128]{2,1,0:T(4,128)} %get-tuple-element.6.tot_h, f32[8,128]{1,0:T(8,128)} %get-tuple-element.7.names_h), custom_call_target="tpu_custom_call" | custom-call | tf_op jit(solution)/shard_map/owner_sums/pallas_call | solution.py:395
